TPU v7x, 32 devices: a whole 2x2x4 slice. The times are simulated.
32 devices in a mesh: blk: 8 (over z, y), clip: 4 (over x, core).
Axes of the slice: x: 2, y: 2, z: 4, core: 2. Of those that a mesh axis runs over, the one named last changes fastest.
Arguments:
- tokens: bfloat16 [4, 16, 128, 1024], P('clip', 'blk'), may hold values from -6 to 6
- noise_levels: int32 [4, 16], P('clip'), may hold values from 0 to 999, as said below
- group_map: int32 [16], replicated, may hold values from 0 to 15, as said below
- noise_table: bfloat16 [1000, 1024], replicated, may hold values from -6 to 6
- mod_weight: bfloat16 [1024, 6144], replicated, may hold values from -0.1875 to 0.1875
- mod_bias: bfloat16 [6144], replicated, may hold values from -3 to 3
- qkv_weight: bfloat16 [1024, 3072], replicated, may hold values from -0.1875 to 0.1875
- out_weight: bfloat16 [1024, 1024], replicated, may hold values from -6 to 6
- fc1_weight: bfloat16 [1024, 4096], replicated, may hold values from -0.1875 to 0.1875
- fc2_weight: bfloat16 [4096, 1024], replicated, may hold values from -0.09375 to 0.09375
- out_cotangent: bfloat16 [4, 16, 128, 1024], P('clip', 'blk'), may hold values from -6 to 6
Outputs:
- layer_out: bfloat16 [4, 16, 128, 1024], P('clip', 'blk')
- tokens_grad: bfloat16 [4, 16, 128, 1024], P('clip', 'blk')
- noise_table_grad: float32 [1000, 1024], P(None, ('blk', 'clip'))
- mod_weight_grad: float32 [1024, 6144], P(('blk', 'clip'))
- mod_bias_grad: float32 [6144], P(('blk', 'clip'))
- qkv_weight_grad: float32 [1024, 3072], P(('blk', 'clip'))
- out_weight_grad: float32 [1024, 1024], P(('blk', 'clip'))
- fc1_weight_grad: float32 [1024, 4096], P(('blk', 'clip'))
- fc2_weight_grad: float32 [4096, 1024], P(('blk', 'clip'))
Inputs may be any that keep to these rules, and one draw needn't show every extreme that they name: `group_map`: A permutation of the frames; slots 2 i and 2 i + 1 hold some frame f and 15 - f, in either order. `noise_levels`: in each clip one frame has level 0 and another level 999.
All inputs are finite; a program needn't handle non-finite values.
Results may differ from a plain program's by a relative error of at most 0.014.
The roundings to bfloat16 on the way count: a program that leaves them out, or rounds other values in their place, can miss the bound.
Values may be sent and summed in bfloat16 or wider, within the bound.
No kernel may reach another device: no remote copies, remote signals or barrier semaphores. Data moves between devices by JAX's collectives and lax.ppermute only.
A program may use at most 256 MiB of HBM per device.

v0:
```python
from functools import partial

import jax
import jax.numpy as jnp
from jax import lax
from jax.sharding import PartitionSpec as P

D = 1024
HEAD = 64
HEADS = 16
LEVELS = 1000
GRID_H = 8
GRID_W = 16
PATCHES = 128


SCALE = 0.125
EPSILON = 1e-06
ROPE_BASE = 10000.0
NEG_LARGE = -1e30


def token_positions(frame_ids):
    slot_count = frame_ids.shape[0]
    total_rows = slot_count * GRID_H * GRID_W
    patch_ids = jnp.arange(total_rows, dtype=jnp.int32) % (GRID_H * GRID_W)
    frame_pos = jnp.repeat(frame_ids, GRID_H * GRID_W, total_repeat_length=total_rows)
    return (frame_pos, patch_ids // GRID_W, patch_ids % GRID_W)


def rope_angles(frame_pos, row_pos, col_pos):
    angle_list = []
    for position, comp_width in ((frame_pos, 16), (row_pos, 24), (col_pos, 24)):
        half_width = comp_width // 2
        frequency = ROPE_BASE ** (-2.0 * jnp.arange(half_width, dtype=jnp.float32) / comp_width)
        angle_list.append(position.astype(jnp.float32)[:, None] * frequency[None, :])
    return angle_list


def rotate(values, angle_list, direction):
    pieces = []
    offset = 0
    for angles in angle_list:
        half_width = angles.shape[1]
        first_half = values[:, :, offset : offset + half_width]
        second_half = values[:, :, offset + half_width : offset + 2 * half_width]
        cosine = jnp.cos(angles)[:, None, :]
        sine_part = direction * jnp.sin(angles)[:, None, :]
        pieces.append(first_half * cosine - second_half * sine_part)
        pieces.append(first_half * sine_part + second_half * cosine)
        offset = offset + 2 * half_width
    return jnp.concatenate(pieces, axis=2)


def normalize(values):
    center = values - jnp.mean(values, axis=-1, keepdims=True)
    inverse = lax.rsqrt(jnp.mean(center * center, axis=-1, keepdims=True) + EPSILON)
    return (center * inverse, inverse)


def norm_backward(grad_in, normed, inverse):
    return inverse * (
        grad_in
        - jnp.mean(grad_in, axis=-1, keepdims=True)
        - normed * jnp.mean(grad_in * normed, axis=-1, keepdims=True)
    )


def frames_of(group_map, first_row, row_count):
    slot_frames = lax.dynamic_slice_in_dim(group_map, first_row // PATCHES, row_count // PATCHES)
    return jnp.repeat(slot_frames, PATCHES, total_repeat_length=row_count)


def block_size(row_count, shard_rows):
    return 2 * shard_rows if row_count // shard_rows % 2 == 0 else shard_rows


def keep_same(values):
    return values


def local(
    tokens,
    noise_levels,
    group_map,
    noise_table,
    mod_weight,
    mod_bias,
    qkv_weight,
    out_weight,
    fc1_weight,
    fc2_weight,
    out_cotangent,
):
    rows_here = 2 * PATCHES
    my_frames = lax.dynamic_slice_in_dim(group_map, 2 * lax.axis_index("blk"), 2)
    frame_hot = (
        jnp.arange(group_map.shape[0], dtype=jnp.int32)[None, :] == my_frames[:, None]
    ).astype(jnp.int32)
    my_levels = jnp.sum(frame_hot * noise_levels[0][None, :], axis=1)
    level_hot = jnp.arange(LEVELS, dtype=jnp.int32)[None, :] == my_levels[:, None]
    embedded = jnp.dot(
        level_hot.astype(jnp.bfloat16), noise_table, preferred_element_type=jnp.float32
    )
    activated = jax.nn.silu(embedded).astype(jnp.bfloat16)
    modulation = (
        jnp.dot(activated, mod_weight, preferred_element_type=jnp.float32)
        + mod_bias.astype(jnp.float32)[None, :]
    )
    shift_one, scale_one, gate_one, shift_two, scale_two, gate_two = [
        modulation[:, member * D : (member + 1) * D][:, None, :] for member in range(6)
    ]
    inputs_here = tokens[0].astype(jnp.float32)
    normed_one, inverse_one = normalize(inputs_here)
    first_in = (
        (normed_one * (1.0 + scale_one) + shift_one).astype(jnp.bfloat16).reshape(rows_here, D)
    )
    qkv_lin = jnp.dot(first_in, qkv_weight, preferred_element_type=jnp.float32)
    token_frames, row_pos, col_pos = token_positions(my_frames)
    angle_list = rope_angles(token_frames, row_pos, col_pos)
    query = rotate(qkv_lin[:, :D].reshape(rows_here, HEADS, HEAD), angle_list, 1.0).astype(
        jnp.bfloat16
    )
    key_part = rotate(
        qkv_lin[:, D : 2 * D].reshape(rows_here, HEADS, HEAD), angle_list, 1.0
    ).astype(jnp.bfloat16)
    value_part = qkv_lin[:, 2 * D :].reshape(rows_here, HEADS, HEAD).astype(jnp.bfloat16)
    top_frame = jnp.max(my_frames)
    own_lowest = jnp.min(my_frames)
    forward_start = (
        jnp.full((HEADS, rows_here), NEG_LARGE, jnp.float32),
        jnp.zeros((HEADS, rows_here), jnp.float32),
        jnp.zeros((rows_here, HEADS, HEAD), jnp.float32),
    )
    first_row = jnp.int32(0)
    keys_piece = lax.all_gather(key_part, "blk", axis=0, tiled=True)
    values_piece = lax.all_gather(value_part, "blk", axis=0, tiled=True)
    piece_rows = keys_piece.shape[0]
    block_rows = block_size(piece_rows, rows_here)

    def forward_advance(turn_index, running):
        offset = turn_index * block_rows
        keys_block = lax.dynamic_slice_in_dim(keys_piece, offset, block_rows)
        values_block = lax.dynamic_slice_in_dim(values_piece, offset, block_rows)
        block_frames = frames_of(group_map, first_row + offset, block_rows)

        def attend(previous):
            top_scores, totals, accumulated = previous
            scores = (
                jnp.einsum("qhd,khd->hqk", query, keys_block, preferred_element_type=jnp.float32)
                * SCALE
            )
            allowed = block_frames[None, None, :] <= token_frames[None, :, None]
            new_top = jnp.maximum(
                top_scores, jnp.max(jnp.where(allowed, scores, NEG_LARGE), axis=2)
            )
            weights = jnp.where(allowed, jnp.exp(scores - new_top[:, :, None]), 0.0)
            factor = jnp.exp(top_scores - new_top)
            update = jnp.einsum(
                "hqk,khd->qhd",
                weights.astype(jnp.bfloat16),
                values_block,
                preferred_element_type=jnp.float32,
            )
            return (
                new_top,
                totals * factor + jnp.sum(weights, axis=2),
                accumulated * factor.T[:, :, None] + update,
            )

        return lax.cond(jnp.min(block_frames) > top_frame, keep_same, attend, running)

    top_scores, totals, accumulated = lax.fori_loop(
        0, piece_rows // block_rows, forward_advance, forward_start
    )
    attended = accumulated / totals.T[:, :, None]
    log_total = top_scores + jnp.log(totals)
    attended_low = attended.astype(jnp.bfloat16).reshape(rows_here, D)
    attn_out = jnp.dot(attended_low, out_weight, preferred_element_type=jnp.float32).reshape(
        2, PATCHES, D
    )
    middle = inputs_here + gate_one * attn_out
    normed_two, inverse_two = normalize(middle)
    second_in = (
        (normed_two * (1.0 + scale_two) + shift_two).astype(jnp.bfloat16).reshape(rows_here, D)
    )
    up_lin = jnp.dot(second_in, fc1_weight, preferred_element_type=jnp.float32)
    hidden = jax.nn.gelu(up_lin, approximate=False).astype(jnp.bfloat16)
    mlp_out = jnp.dot(hidden, fc2_weight, preferred_element_type=jnp.float32).reshape(2, PATCHES, D)
    layer_out = (middle + gate_two * mlp_out).astype(jnp.bfloat16)[None]
    cotangent = out_cotangent[0].astype(jnp.float32)
    d_gate_two = jnp.sum(cotangent * mlp_out, axis=1)
    d_mlp = (cotangent * gate_two).astype(jnp.bfloat16).reshape(rows_here, D)
    lower_part = jnp.einsum("rf,rd->fd", hidden, d_mlp, preferred_element_type=jnp.float32)
    d_hidden = jnp.einsum("rd,fd->rf", d_mlp, fc2_weight, preferred_element_type=jnp.float32)
    unused_value, gelu_pull = jax.vjp(partial(jax.nn.gelu, approximate=False), up_lin)
    d_up = gelu_pull(d_hidden)[0].astype(jnp.bfloat16)
    upper_part = jnp.einsum("rc,rf->cf", second_in, d_up, preferred_element_type=jnp.float32)
    d_second = jnp.einsum(
        "rf,cf->rc", d_up, fc1_weight, preferred_element_type=jnp.float32
    ).reshape(2, PATCHES, D)
    d_shift_two = jnp.sum(d_second, axis=1)
    d_scale_two = jnp.sum(d_second * normed_two, axis=1)
    d_middle = cotangent + norm_backward(d_second * (1.0 + scale_two), normed_two, inverse_two)
    d_gate_one = jnp.sum(d_middle * attn_out, axis=1)
    d_attn = (d_middle * gate_one).astype(jnp.bfloat16).reshape(rows_here, D)
    outw_part = jnp.einsum("rc,rd->cd", attended_low, d_attn, preferred_element_type=jnp.float32)
    d_attended = (
        jnp.einsum("rd,cd->rc", d_attn, out_weight, preferred_element_type=jnp.float32)
        .astype(jnp.bfloat16)
        .reshape(rows_here, HEADS, HEAD)
    )
    delta = jnp.sum(d_attended.astype(jnp.float32) * attended, axis=2).T
    grad_start = jnp.zeros((rows_here, HEADS, HEAD), jnp.float32)
    query_first_row = jnp.int32(0)
    query_keys_piece = lax.all_gather(key_part, "blk", axis=0, tiled=True)
    query_values_piece = lax.all_gather(value_part, "blk", axis=0, tiled=True)
    piece_rows = query_keys_piece.shape[0]
    query_block_rows = block_size(piece_rows, rows_here)

    def query_advance(turn_index, running):
        offset = turn_index * query_block_rows
        keys_block = lax.dynamic_slice_in_dim(query_keys_piece, offset, query_block_rows)
        values_block = lax.dynamic_slice_in_dim(query_values_piece, offset, query_block_rows)
        block_frames = frames_of(group_map, query_first_row + offset, query_block_rows)

        def query_accumulate(previous):
            scores = (
                jnp.einsum("qhd,khd->hqk", query, keys_block, preferred_element_type=jnp.float32)
                * SCALE
            )
            allowed = block_frames[None, None, :] <= token_frames[None, :, None]
            weights = jnp.where(allowed, jnp.exp(scores - log_total[:, :, None]), 0.0)
            weight_grad = jnp.einsum(
                "qhd,khd->hqk", d_attended, values_block, preferred_element_type=jnp.float32
            )
            score_grad = (weights * (weight_grad - delta[:, :, None]) * SCALE).astype(jnp.bfloat16)
            return previous + jnp.einsum(
                "hqk,khd->qhd", score_grad, keys_block, preferred_element_type=jnp.float32
            )

        return lax.cond(jnp.min(block_frames) > top_frame, keep_same, query_accumulate, running)

    query_grad = lax.fori_loop(0, piece_rows // query_block_rows, query_advance, grad_start)
    stats_lse, stats_delta = (
        lax.all_gather(log_total.T, "blk", axis=0, tiled=True),
        lax.all_gather(delta.T, "blk", axis=0, tiled=True),
    )
    key_first_row = jnp.int32(0)
    queries_piece = lax.all_gather(query, "blk", axis=0, tiled=True)
    grads_piece = lax.all_gather(d_attended, "blk", axis=0, tiled=True)
    piece_rows = queries_piece.shape[0]
    key_block_rows = block_size(piece_rows, rows_here)

    def key_advance(turn_index, running):
        offset = turn_index * key_block_rows
        query_block = lax.dynamic_slice_in_dim(queries_piece, offset, key_block_rows)
        grad_block = lax.dynamic_slice_in_dim(grads_piece, offset, key_block_rows)
        lse_block = lax.dynamic_slice_in_dim(stats_lse, key_first_row + offset, key_block_rows).T
        delta_block = lax.dynamic_slice_in_dim(
            stats_delta, key_first_row + offset, key_block_rows
        ).T
        block_frames = frames_of(group_map, key_first_row + offset, key_block_rows)

        def key_accumulate(previous):
            key_total, value_total = previous
            scores = (
                jnp.einsum(
                    "qhd,khd->hqk", query_block, key_part, preferred_element_type=jnp.float32
                )
                * SCALE
            )
            allowed = token_frames[None, None, :] <= block_frames[None, :, None]
            weights = jnp.where(allowed, jnp.exp(scores - lse_block[:, :, None]), 0.0)
            value_total = value_total + jnp.einsum(
                "hqk,qhd->khd",
                weights.astype(jnp.bfloat16),
                grad_block,
                preferred_element_type=jnp.float32,
            )
            weight_grad = jnp.einsum(
                "qhd,khd->hqk", grad_block, value_part, preferred_element_type=jnp.float32
            )
            score_grad = (weights * (weight_grad - delta_block[:, :, None]) * SCALE).astype(
                jnp.bfloat16
            )
            key_total = key_total + jnp.einsum(
                "hqk,qhd->khd", score_grad, query_block, preferred_element_type=jnp.float32
            )
            return (key_total, value_total)

        return lax.cond(jnp.max(block_frames) < own_lowest, keep_same, key_accumulate, running)

    key_grad, value_grad = lax.fori_loop(
        0, piece_rows // key_block_rows, key_advance, (grad_start, grad_start)
    )
    query_low = lax.optimization_barrier(query_grad.astype(jnp.bfloat16)).astype(jnp.float32)
    key_low = lax.optimization_barrier(key_grad.astype(jnp.bfloat16)).astype(jnp.float32)
    query_back = rotate(query_low, angle_list, -1.0).reshape(rows_here, D)
    key_back = rotate(key_low, angle_list, -1.0).reshape(rows_here, D)
    d_qkv = jnp.concatenate(
        [query_back, key_back, value_grad.reshape(rows_here, D)], axis=1
    ).astype(jnp.bfloat16)
    qkv_part = jnp.einsum("rc,rk->ck", first_in, d_qkv, preferred_element_type=jnp.float32)
    d_first = jnp.einsum(
        "rk,ck->rc", d_qkv, qkv_weight, preferred_element_type=jnp.float32
    ).reshape(2, PATCHES, D)
    d_shift_one = jnp.sum(d_first, axis=1)
    d_scale_one = jnp.sum(d_first * normed_one, axis=1)
    tokens_grad = (
        d_middle + norm_backward(d_first * (1.0 + scale_one), normed_one, inverse_one)
    ).astype(jnp.bfloat16)[None]
    d_mod = jnp.concatenate(
        [d_shift_one, d_scale_one, d_gate_one, d_shift_two, d_scale_two, d_gate_two], axis=1
    )
    bias_part = jnp.sum(d_mod, axis=0)
    d_mod_low = d_mod.astype(jnp.bfloat16)
    d_activated = jnp.einsum("sk,ck->sc", d_mod_low, mod_weight, preferred_element_type=jnp.float32)
    unused_silu, silu_pull = jax.vjp(jax.nn.silu, embedded)
    d_embedded = silu_pull(d_activated)[0]
    table_part = jnp.einsum(
        "sl,sc->cl", level_hot.astype(jnp.float32), d_embedded, precision=lax.Precision.HIGHEST
    )
    activated_all, d_mod_all = (
        lax.all_gather(activated, ("blk", "clip"), axis=0, tiled=True),
        lax.all_gather(d_mod_low, ("blk", "clip"), axis=0, tiled=True),
    )
    share_rows = D // lax.axis_size(("blk", "clip"))
    my_columns = lax.dynamic_slice_in_dim(
        activated_all, lax.axis_index(("blk", "clip")) * share_rows, share_rows, 1
    )
    modw_share = jnp.einsum("sc,sk->ck", my_columns, d_mod_all, preferred_element_type=jnp.float32)
    summed = (
        lax.psum_scatter(table_part, ("blk", "clip"), scatter_dimension=0, tiled=True),
        lax.psum_scatter(bias_part, ("blk", "clip"), scatter_dimension=0, tiled=True),
        lax.psum_scatter(qkv_part, ("blk", "clip"), scatter_dimension=0, tiled=True),
        lax.psum_scatter(outw_part, ("blk", "clip"), scatter_dimension=0, tiled=True),
        lax.psum_scatter(upper_part, ("blk", "clip"), scatter_dimension=0, tiled=True),
        lax.psum_scatter(lower_part, ("blk", "clip"), scatter_dimension=0, tiled=True),
    )
    return (
        layer_out,
        tokens_grad,
        summed[0].T,
        modw_share,
        summed[1],
        summed[2],
        summed[3],
        summed[4],
        summed[5],
    )


def solution(mesh):
    return jax.shard_map(
        local,
        mesh=mesh,
        in_specs=(
            P("clip", "blk", None, None),
            P("clip", None),
            P(),
            P(),
            P(),
            P(),
            P(),
            P(),
            P(),
            P(),
            P("clip", "blk", None, None),
        ),
        out_specs=(
            P("clip", "blk", None, None),
            P("clip", "blk", None, None),
            P(None, ("blk", "clip")),
            P(("blk", "clip"), None),
            P(("blk", "clip")),
            P(("blk", "clip"), None),
            P(("blk", "clip"), None),
            P(("blk", "clip"), None),
            P(("blk", "clip"), None),
        ),
        check_vma=False,
    )
```

profile of v0, /device:TPU:0, one launch (start us, length us, event | category | flops | bytes accessed | tf_op | source)
XLA Modules:
  0.0 1269.2 jit_solution(14010569110282314404)
XLA Ops:
  55.5 66.4 %all-gather.7.cloned.1.call-done = bf16[2048,16,64]{0,2,1:T(8,128)(2,1)} async-done(((bf16[256,16,64]{0,2,1:T(8,128)(2,1)}), bf16[2048,16,64]{0,2,1:T(8,128)(2,1)}) %all-gather.7.cloned.1.call-update) | async-done | bytes 4194320 | tf_op jit(solution)/shard_map/all_gather | solution.py:136
  121.9 75.8 %all-gather.9.cloned.1.call-done = bf16[2048,16,64]{0,2,1:T(8,128)(2,1)} async-done(((bf16[256,16,64]{0,2,1:T(8,128)(2,1)}), bf16[2048,16,64]{0,2,1:T(8,128)(2,1)}) %all-gather.9.cloned.1.call-update) | async-done | bytes 4194320 | tf_op jit(solution)/shard_map/all_gather | solution.py:137
  198.9 58.5 %while.67 = (s32[]{:T(128)}, f32[16,256]{1,0:T(8,128)S(1)}, f32[16,256]{1,0:T(8,128)S(1)}, f32[256,16,64]{0,2,1:T(8,128)}, s32[16]{0:T(128)S(1)}, /*index=5*/s32...) while((s32[]{:T(128)}, f32[16,256]{1,0:T(8,128)S(1)}, ...), condition=%wide.region_10.12_spmd.clone, body=%wide.region_4.11_spmd.clone.sunk | while | flops 560619776 | bytes 39077608 | solution.py:173
  205.3 8.2 conditional.9
  268.3 13.5 %add_convert_fusion = (bf16[256,4096]{1,0:T(8,128)(2,1)S(1)}, f32[256,4096]{1,0:T(8,128)S(1)}) fusion(f32[256,4096]{1,0:T(8,128)S(1)} %fusion.163, bf16[256,1024]{1,0:T(8,128)(2,1)S(1)} %copy-done.23, bf16[4096,1024]{1,0:T(8,128)(2,1)S(1)} %bitcast.388), kind=kOutput, calls=%fused_computation.106 | convolution fusion | flops 2222981120 | bytes 19398656 | tf_op jit(solution)/shard_map/rd,fd->rf/dot_general | solution.py:195
  306.7 79.7 %while.68 = (s32[]{:T(128)}, f32[256,16,64]{0,2,1:T(8,128)S(1)}, s32[16]{0:T(128)S(1)}, s32[]{:T(128)}, bf16[2048,16,64]{0,2,1:T(8,128)(2,1)}, /*index=5*/bf16[2...) while((s32[]{:T(128)}, f32[256,16,64]{0,2,1:T(8,128)S(1)}, ...), condition=%wide.region_20.22_spmd.clone, body=%wide.region_16.21_spmd.clone.sunk | while | flops 820392192 | bytes 23382680 | solution.py:244
  313.3 13.5 %conditional.10 = (f32[256,16,64]{0,2,1:T(8,128)S(1)}) conditional(s32[]{:T(128)} %convert_element_type.359, (s32[512]{0:T(512)S(1)}, s32[256]{0:T(256)S(1)}, s32[]{:T(128)}, pred[]{:T(512)}, bf16[2048,16,64]{0,2,1:T(8,128)(2,1)}, /*index=5*/bf16[256,16,64]{0,2,1:T(8,128)(2,1)S(1)}, f32[16,256]{1,0:T(8,128)S(1)}, bf16[2048,16,64]{0,2,1:T(8,128)(2,1)}, ...), branch_computations={%region_18.19_spmd, %region_19.20_spmd} | conditional | flops 820380672 | bytes 23372844 | solution.py:242
  333.1 13.5 %conditional.10 = (f32[256,16,64]{0,2,1:T(8,128)S(1)}) conditional(s32[]{:T(128)} %convert_element_type.359, (s32[512]{0:T(512)S(1)}, s32[256]{0:T(256)S(1)}, s32[]{:T(128)}, pred[]{:T(512)}, bf16[2048,16,64]{0,2,1:T(8,128)(2,1)}, /*index=5*/bf16[256,16,64]{0,2,1:T(8,128)(2,1)S(1)}, f32[16,256]{1,0:T(8,128)S(1)}, bf16[2048,16,64]{0,2,1:T(8,128)(2,1)}, ...), branch_computations={%region_18.19_spmd, %region_19.20_spmd} | conditional | flops 820380672 | bytes 23372844 | solution.py:242
  353.0 13.6 %conditional.10 = (f32[256,16,64]{0,2,1:T(8,128)S(1)}) conditional(s32[]{:T(128)} %convert_element_type.359, (s32[512]{0:T(512)S(1)}, s32[256]{0:T(256)S(1)}, s32[]{:T(128)}, pred[]{:T(512)}, bf16[2048,16,64]{0,2,1:T(8,128)(2,1)}, /*index=5*/bf16[256,16,64]{0,2,1:T(8,128)(2,1)S(1)}, f32[16,256]{1,0:T(8,128)S(1)}, bf16[2048,16,64]{0,2,1:T(8,128)(2,1)}, ...), branch_computations={%region_18.19_spmd, %region_19.20_spmd} | conditional | flops 820380672 | bytes 23372844 | solution.py:242
  372.9 13.5 %conditional.10 = (f32[256,16,64]{0,2,1:T(8,128)S(1)}) conditional(s32[]{:T(128)} %convert_element_type.359, (s32[512]{0:T(512)S(1)}, s32[256]{0:T(256)S(1)}, s32[]{:T(128)}, pred[]{:T(512)}, bf16[2048,16,64]{0,2,1:T(8,128)(2,1)}, /*index=5*/bf16[256,16,64]{0,2,1:T(8,128)(2,1)S(1)}, f32[16,256]{1,0:T(8,128)S(1)}, bf16[2048,16,64]{0,2,1:T(8,128)(2,1)}, ...), branch_computations={%region_18.19_spmd, %region_19.20_spmd} | conditional | flops 820380672 | bytes 23372844 | solution.py:242
  386.7 30.6 %all_gather.29 = f32[2048,16]{0,1:T(8,128)S(1)} all-gather(f32[256,16]{0,1:T(8,128)S(1)} %bitcast.376), channel_id=1, replica_groups=mesh['blk'=8,'clip'=4] {'blk'}, dimensions={0}, use_global_device_ids=true | all-gather | bytes 147456 | tf_op jit(solution)/shard_map/all_gather | solution.py:247
  417.2 30.6 %all_gather.28 = f32[2048,16]{0,1:T(8,128)S(1)} all-gather(f32[256,16]{0,1:T(8,128)S(1)} %bitcast.377), channel_id=1, replica_groups=mesh['blk'=8,'clip'=4] {'blk'}, dimensions={0}, use_global_device_ids=true | all-gather | bytes 147456 | tf_op jit(solution)/shard_map/all_gather | solution.py:246
  449.9 109.1 %while.69 = (s32[]{:T(128)}, f32[256,16,64]{0,2,1:T(8,128)S(1)}, f32[256,16,64]{0,2,1:T(8,128)}, s32[16]{0:T(128)}, s32[]{:T(128)}, /*index=5*/f32[2048,16]{0,1:...) while((s32[]{:T(128)}, f32[256,16,64]{0,2,1:T(8,128)S(1)}, ...), condition=%wide.region_26.28_spmd.clone, body=%wide.region_22.27_spmd.clone.sunk | while | flops 1097478400 | bytes 35245768 | solution.py:294
  457.1 20.4 %conditional.11 = ((f32[256,16,64]{0,2,1:T(8,128)S(1)}, f32[256,16,64]{0,2,1:T(8,128)})) conditional(s32[]{:T(128)} %convert_element_type.360, (s32[256]{0:T(256)S(1)}, s32[512]{0:T(512)S(1)}, bf16[2048,16,64]{0,2,1:T(8,128)(2,1)}, s32[]{:T(128)}, bf16[256,16,64]{0,2,1:T(8,128)(2,1)S(1)}, /*index=5*/f32[16,512]{1,0:T(8,128)S(1)}, ...), branch_computations={%region_24.25_spmd, %region_25.26_spmd} | conditional | flops 1097466880 | bytes 35104800 | solution.py:292
  484.4 20.3 %conditional.11 = ((f32[256,16,64]{0,2,1:T(8,128)S(1)}, f32[256,16,64]{0,2,1:T(8,128)})) conditional(s32[]{:T(128)} %convert_element_type.360, (s32[256]{0:T(256)S(1)}, s32[512]{0:T(512)S(1)}, bf16[2048,16,64]{0,2,1:T(8,128)(2,1)}, s32[]{:T(128)}, bf16[256,16,64]{0,2,1:T(8,128)(2,1)S(1)}, /*index=5*/f32[16,512]{1,0:T(8,128)S(1)}, ...), branch_computations={%region_24.25_spmd, %region_25.26_spmd} | conditional | flops 1097466880 | bytes 35104800 | solution.py:292
  511.7 20.2 %conditional.11 = ((f32[256,16,64]{0,2,1:T(8,128)S(1)}, f32[256,16,64]{0,2,1:T(8,128)})) conditional(s32[]{:T(128)} %convert_element_type.360, (s32[256]{0:T(256)S(1)}, s32[512]{0:T(512)S(1)}, bf16[2048,16,64]{0,2,1:T(8,128)(2,1)}, s32[]{:T(128)}, bf16[256,16,64]{0,2,1:T(8,128)(2,1)S(1)}, /*index=5*/f32[16,512]{1,0:T(8,128)S(1)}, ...), branch_computations={%region_24.25_spmd, %region_25.26_spmd} | conditional | flops 1097466880 | bytes 35104800 | solution.py:292
  538.8 20.2 %conditional.11 = ((f32[256,16,64]{0,2,1:T(8,128)S(1)}, f32[256,16,64]{0,2,1:T(8,128)})) conditional(s32[]{:T(128)} %convert_element_type.360, (s32[256]{0:T(256)S(1)}, s32[512]{0:T(512)S(1)}, bf16[2048,16,64]{0,2,1:T(8,128)(2,1)}, s32[]{:T(128)}, bf16[256,16,64]{0,2,1:T(8,128)(2,1)S(1)}, /*index=5*/f32[16,512]{1,0:T(8,128)S(1)}, ...), branch_computations={%region_24.25_spmd, %region_25.26_spmd} | conditional | flops 1097466880 | bytes 35104800 | solution.py:292
  561.3 8.7 concatenate.51
  618.4 39.0 %all-gather = bf16[32,2,1024]{2,1,0:T(2,128)(2,1)S(1)} all-gather(bf16[1,2,1024]{2,1,0:T(2,128)(2,1)S(1)} %fusion.152), channel_id=1, replica_groups=mesh['blk'=8,'clip'=4] {'blk','clip'}, dimensions={0}, use_global_device_ids=true | all-gather | bytes 135168 | tf_op jit(solution)/shard_map/all_gather | solution.py:325
  657.5 41.9 %all-gather.1 = bf16[32,2,6144]{2,1,0:T(2,128)(2,1)} all-gather(bf16[1,2,6144]{2,1,0:T(2,128)(2,1)S(1)} %get-tuple-element.1893), channel_id=1, replica_groups=mesh['blk'=8,'clip'=4] {'blk','clip'}, dimensions={0}, use_global_device_ids=true | all-gather | bytes 811008 | tf_op jit(solution)/shard_map/all_gather | solution.py:326
  701.8 37.5 %all-reduce = f32[6144]{0:T(1024)S(1)} all-reduce(f32[6144]{0:T(1024)S(1)} %get-tuple-element.1892), channel_id=3, replica_groups=mesh['blk'=8,'clip'=4] {'blk','clip'}, use_global_device_ids=true, to_apply=%region_37.39.clone | all-reduce | flops 6144 | bytes 49152
  741.1 148.9 %reduce-scatter.8.cloned.1.call-done = f32[32,3072]{1,0:T(8,128)} async-done(((f32[1024,3072]{1,0:T(8,128)}), f32[32,3072]{1,0:T(8,128)}) %reduce-scatter.8.cloned.1.call-update) | async-done | bytes 393232 | tf_op jit(solution)/shard_map/reduce_scatter | solution.py:336
  890.0 184.9 %reduce-scatter.12.cloned.1.call-done = f32[32,4096]{1,0:T(8,128)} async-done(((f32[1024,4096]{1,0:T(8,128)}), f32[32,4096]{1,0:T(8,128)}) %reduce-scatter.12.cloned.1.call-update) | async-done | bytes 524304 | tf_op jit(solution)/shard_map/reduce_scatter | solution.py:338
  1075.0 187.5 %reduce-scatter.14.cloned.1.call-done = f32[128,1024]{1,0:T(8,128)} async-done(((f32[4096,1024]{1,0:T(8,128)}), f32[128,1024]{1,0:T(8,128)}) %reduce-scatter.14.cloned.1.call-update) | async-done | bytes 524304 | tf_op jit(solution)/shard_map/reduce_scatter | solution.py:339
  (417 shorter events, 396.1 us)
Async XLA Ops:
  7.2 252.5 %copy-start = (bf16[1024,1024]{1,0:T(8,128)(2,1)S(1)}, bf16[1024,1024]{1,0:T(8,128)(2,1)}, u32[]{:S(2)}) copy-start(bf16[1024,1024]{1,0:T(8,128)(2,1)} %param.40) | copy-start | bytes 6291460
  7.2 114.7 %all-gather.7.cloned.1.call-start = ((), (), s32[]{:S(2)}) async-start(), calls=%async_computation.5 | async-start | bytes 4718592 | tf_op jit(solution)/shard_map/all_gather | solution.py:136
  11.0 11.4 slice-start.2
  34.3 13.5 %copy-start.28 = (f32[256,12]{0,1:T(8,128)}, f32[256,12]{0,1:T(8,128)S(1)}, u32[]{:S(2)}) copy-start(f32[256,12]{0,1:T(8,128)S(1)} %get-tuple-element.1905) | copy-start | bytes 36868
  34.3 13.5 %copy-start.30 = (f32[256,12]{0,1:T(8,128)}, f32[256,12]{0,1:T(8,128)S(1)}, u32[]{:S(2)}) copy-start(f32[256,12]{0,1:T(8,128)S(1)} %get-tuple-element.1917) | copy-start | bytes 36868
  37.0 161.8 %copy-start.52 = (s32[16]{0:T(128)S(1)}, s32[16]{0:T(128)}, u32[]{:S(2)}) copy-start(s32[16]{0:T(128)} %param.35) | copy-start | bytes 196
  44.0 153.7 %all-gather.9.cloned.1.call-start = ((), (), s32[]{:S(2)}) async-start(), calls=%async_computation.6 | async-start | bytes 4718592 | tf_op jit(solution)/shard_map/all_gather | solution.py:137
  46.4 402.3 %all-gather.11.cloned.1.call-start = ((), (), s32[]{:S(2)}) async-start(), calls=%async_computation.7 | async-start | bytes 4718592 | tf_op jit(solution)/shard_map/all_gather | solution.py:250
  54.9 393.8 %all-gather.13.cloned.1.call-start = ((), (), s32[]{:S(2)}) async-start(), calls=%async_computation.8 | async-start | bytes 4718592 | tf_op jit(solution)/shard_map/all_gather | solution.py:251
  262.3 19.5 %slice-start = ((s8[8388608]{0:T(1024)(128)(4,1)}), s8[4194304]{0:T(1024)(128)(4,1)S(1)}, s32[]{:S(2)}) async-start(s8[8388608]{0:T(1024)(128)(4,1)} %bitcast.347), calls=%async_computation.14 | async-start | bytes 8388608
  268.3 13.5 %slice-start.1 = ((s8[8388608]{0:T(1024)(128)(4,1)}), s8[4194304]{0:T(1024)(128)(4,1)S(1)}, s32[]{:S(2)}) async-start(s8[8388608]{0:T(1024)(128)(4,1)} %bitcast.347), calls=%async_computation.15 | async-start | bytes 8388608
  300.2 440.9 %reduce-scatter.10.cloned.1.call-start = ((), (), s32[]{:S(2)}) async-start(), calls=%async_computation.11 | async-start | bytes 4325376 | tf_op jit(solution)/shard_map/reduce_scatter | solution.py:337
  305.4 435.7 %reduce-scatter.6.cloned.1.call-start = ((), (), s32[]{:S(2)}) async-start(), calls=%async_computation.9 | async-start | bytes 4325376 | tf_op jit(solution)/shard_map/reduce_scatter | solution.py:334
  306.7 141.1 %copy-start.29 = (f32[256,12]{0,1:T(8,128)S(1)}, f32[256,12]{0,1:T(8,128)}, u32[]{:S(2)}) copy-start(f32[256,12]{0,1:T(8,128)} %copy-done.28) | copy-start | bytes 36868
  306.7 141.1 %copy-start.31 = (f32[256,12]{0,1:T(8,128)S(1)}, f32[256,12]{0,1:T(8,128)}, u32[]{:S(2)}) copy-start(f32[256,12]{0,1:T(8,128)} %copy-done.30) | copy-start | bytes 36868
  306.7 141.1 %copy-start.34 = (f32[256,12]{0,1:T(8,128)S(1)}, f32[256,12]{0,1:T(8,128)}, u32[]{:S(2)}) copy-start(f32[256,12]{0,1:T(8,128)} %get-tuple-element.1904) | copy-start | bytes 36868
  306.7 141.1 %copy-start.35 = (f32[256,12]{0,1:T(8,128)S(1)}, f32[256,12]{0,1:T(8,128)}, u32[]{:S(2)}) copy-start(f32[256,12]{0,1:T(8,128)} %get-tuple-element.1919) | copy-start | bytes 36868
  386.5 61.4 %copy-start.53 = (s32[16]{0:T(128)}, s32[16]{0:T(128)S(1)}, u32[]{:S(2)}) copy-start(s32[16]{0:T(128)S(1)} %get-tuple-element.2430) | copy-start | bytes 196
  386.5 63.4 %copy-start.3 = (bf16[256,16,64]{0,2,1:T(8,128)(2,1)S(1)}, bf16[256,16,64]{0,2,1:T(8,128)(2,1)}, u32[]{:S(2)}) copy-start(bf16[256,16,64]{0,2,1:T(8,128)(2,1)} %concatenate.49) | copy-start | bytes 1572868
  559.1 14.7 %copy-start.5 = (bf16[1,2,128,1024]{3,2,1,0:T(8,128)(2,1)S(1)}, bf16[1,2,128,1024]{3,2,1,0:T(8,128)(2,1)}, u32[]{:S(2)}) copy-start(bf16[1,2,128,1024]{3,2,1,0:T(8,128)(2,1)} %param.33) | copy-start | bytes 1572868
  592.2 297.8 %reduce-scatter.8.cloned.1.call-start = ((), (), s32[]{:S(2)}) async-start(), calls=%async_computation.10 | async-start | bytes 12976128 | tf_op jit(solution)/shard_map/reduce_scatter | solution.py:336
  598.7 476.3 %reduce-scatter.12.cloned.1.call-start = ((), (), s32[]{:S(2)}) async-start(), calls=%async_computation.12 | async-start | bytes 17301504 | tf_op jit(solution)/shard_map/reduce_scatter | solution.py:338
  608.5 653.9 %reduce-scatter.14.cloned.1.call-start = ((), (), s32[]{:S(2)}) async-start(), calls=%async_computation.13 | async-start | bytes 17301504 | tf_op jit(solution)/shard_map/reduce_scatter | solution.py:339
  618.3 644.1 %copy-start.1 = (bf16[1024,1024]{1,0:T(8,128)(2,1)S(1)}, bf16[1024,1024]{1,0:T(8,128)(2,1)}, u32[]{:S(2)}) copy-start(bf16[1024,1024]{1,0:T(8,128)(2,1)} %param.40) | copy-start | bytes 6291460
  (51 other events, 203.8 us)
Sparse Core Ops, SparseCore 0:
  44.1 77.7 all-gather.6
  124.5 73.1 all-gather.8
  200.4 73.1 all-gather.10
  300.3 73.1 all-gather.12
  376.2 139.1 reduce-scatter.9
  592.4 139.5 reduce-scatter.5
  738.5 151.4 reduce-scatter.7
  893.0 181.9 reduce-scatter.11
  1078.0 184.4 reduce-scatter.13
where the time goes:
time: 1280 us; the launch traced here: 1270 us
  waiting for transfers between devices  664 us (52%)
  matrix products  245 us (19%)
  blocking collectives  180 us (14%)
  other arithmetic  85.5 us (7%)
  local copies, waits for them, and re-layouts  61.9 us (5%)
  loops' own time  17.1 us (1%)
  between operations  15 us (1%)
    reduce_scatter x1, waiting for transfers between devices, local(): lax.psum_scatter(lower_part, ('blk', 'clip'), scatter_dimension=0, tiled=...  187 us
    reduce_scatter x1, waiting for transfers between devices, local(): lax.psum_scatter(upper_part, ('blk', 'clip'), scatter_dimension=0, tiled=...  185 us
    reduce_scatter x1, waiting for transfers between devices, local(): lax.psum_scatter(qkv_part, ('blk', 'clip'), scatter_dimension=0, tiled=True)  149 us
    all_gather x1, waiting for transfers between devices, local(): values_piece = lax.all_gather(value_part, 'blk', axis=0, tiled=True)  75.8 us
    all_gather x1, waiting for transfers between devices, local(): keys_piece = lax.all_gather(key_part, 'blk', axis=0, tiled=True)  66.4 us
    all_gather x1, blocking collectives, local(): lax.all_gather(d_mod_low, ('blk', 'clip'), axis=0, tiled=True)  41.9 us
    all_gather x1, blocking collectives, local(): lax.all_gather(activated, ('blk', 'clip'), axis=0, tiled=True)  39 us
    select_n x12, other arithmetic, frames_of(): return jnp.repeat(slot_frames, PATCHES, total_repeat_length=row_count)  37.7 us
  transfers between devices with their start and end apart: 9, of which 5 were waited for; matrix products, arithmetic and copies ran while one was open for 28% of the time, Pallas kernels for 0%

commit v1 on v0

--- a/solution.py
+++ b/solution.py
@@ -3,6 +3,8 @@
 import jax
 import jax.numpy as jnp
 from jax import lax
+from jax.experimental import pallas as pl
+from jax.experimental.pallas import tpu as pltpu
 from jax.sharding import PartitionSpec as P
 
 D = 1024
@@ -351,9 +353,535 @@
     )
 
 
+LANES = 128
+FF = 4096
+AXES = ("blk", "clip")
+EXP_SCALE = SCALE * 1.4426950408889634
+VMEM_LIMIT = 56 * 1024 * 1024
+NT = (((1,), (1,)), ((), ()))
+NN = (((1,), (0,)), ((), ()))
+
+
+def full_block(shape):
+    return pl.BlockSpec(shape, lambda *ids: (0,) * len(shape))
+
+
+def rope_tables(frame_count):
+    lane = jnp.arange(LANES, dtype=jnp.int32) % HEAD
+    pieces = []
+    for comp_width in (16, 24, 24):
+        half_width = comp_width // 2
+        frequency = ROPE_BASE ** (-2.0 * jnp.arange(half_width, dtype=jnp.float32) / comp_width)
+        pieces += [frequency, frequency]
+    frequency = jnp.tile(jnp.concatenate(pieces), LANES // HEAD)[None, :]
+    first = (lane < 8) | ((lane >= 16) & (lane < 28)) | ((lane >= 40) & (lane < 52))
+    sign = jnp.where(first, -1.0, 1.0)[None, :]
+    in_frame = (lane < 16)[None, :]
+    in_row = (lane < 40)[None, :]
+    frame_angle = jnp.arange(frame_count, dtype=jnp.float32)[:, None] * frequency
+    patch = jnp.arange(PATCHES, dtype=jnp.int32)[:, None]
+    place = jnp.where(in_row, patch // GRID_W, patch % GRID_W).astype(jnp.float32)
+    place_angle = place * frequency
+    return (
+        jnp.where(in_frame, jnp.cos(frame_angle), 0.0),
+        jnp.where(in_frame, sign * jnp.sin(frame_angle), 0.0),
+        jnp.where(in_frame, 0.0, jnp.cos(place_angle)),
+        jnp.where(in_frame, 0.0, sign * jnp.sin(place_angle)),
+    )
+
+
+def partner_lanes(values):
+    lane = lax.broadcasted_iota(jnp.int32, values.shape, 1) % HEAD
+    ahead_eight = pltpu.roll(values, LANES - 8, 1)
+    behind_eight = pltpu.roll(values, 8, 1)
+    ahead_twelve = pltpu.roll(values, LANES - 12, 1)
+    behind_twelve = pltpu.roll(values, 12, 1)
+    ahead = ((lane >= 16) & (lane < 28)) | ((lane >= 40) & (lane < 52))
+    return jnp.where(
+        lane < 8,
+        ahead_eight,
+        jnp.where(lane < 16, behind_eight, jnp.where(ahead, ahead_twelve, behind_twelve)),
+    )
+
+
+def qkv_kernel(
+    frames_ref,
+    tokens_ref,
+    mod_ref,
+    qw_ref,
+    kw_ref,
+    vw_ref,
+    fcos_ref,
+    fsin_ref,
+    pcos_ref,
+    psin_ref,
+    out_ref,
+    first_ref,
+):
+    @pl.when(pl.program_id(0) == 0)
+    def _():
+        for slot in range(2):
+            rows = slice(slot * PATCHES, (slot + 1) * PATCHES)
+            normed, unused = normalize(tokens_ref[rows, :].astype(jnp.float32))
+            shift = mod_ref[slot : slot + 1, :D]
+            scale = mod_ref[slot : slot + 1, D : 2 * D]
+            first_ref[rows, :] = (normed * (1.0 + scale) + shift).astype(jnp.bfloat16)
+
+    first = first_ref[...]
+    linear = [
+        lax.dot_general(first, ref[...], NN, preferred_element_type=jnp.float32)
+        for ref in (qw_ref, kw_ref, vw_ref)
+    ]
+    for slot in range(2):
+        rows = slice(slot * PATCHES, (slot + 1) * PATCHES)
+        frame = frames_ref[slot]
+        cosine = pcos_ref[...] + fcos_ref[pl.ds(frame, 1), :]
+        sine = psin_ref[...] + fsin_ref[pl.ds(frame, 1), :]
+        for part in range(2):
+            values = linear[part][rows, :]
+            turned = values * cosine + partner_lanes(values) * sine
+            out_ref[0, rows, part * LANES : (part + 1) * LANES] = turned.astype(jnp.bfloat16)
+        out_ref[0, rows, 2 * LANES :] = linear[2][rows, :].astype(jnp.bfloat16)
+
+
+def project_qkv(my_frames, tokens_here, mod_first, qkv_weight, tables):
+    groups = D // LANES
+    rows = tokens_here.shape[0]
+    weight_specs = [
+        pl.BlockSpec((D, LANES), lambda g, frames, part=part: (0, part * groups + g))
+        for part in range(3)
+    ]
+    return pl.pallas_call(
+        qkv_kernel,
+        grid_spec=pltpu.PrefetchScalarGridSpec(
+            num_scalar_prefetch=1,
+            grid=(groups,),
+            in_specs=[full_block((rows, D)), full_block(mod_first.shape)]
+            + weight_specs
+            + [full_block(table.shape) for table in tables],
+            out_specs=[
+                pl.BlockSpec((1, rows, 3 * LANES), lambda g, frames: (g, 0, 0)),
+                full_block((rows, D)),
+            ],
+        ),
+        out_shape=[
+            jax.ShapeDtypeStruct((groups, rows, 3 * LANES), jnp.bfloat16),
+            jax.ShapeDtypeStruct((rows, D), jnp.bfloat16),
+        ],
+        compiler_params=pltpu.CompilerParams(
+            vmem_limit_bytes=VMEM_LIMIT, dimension_semantics=("arbitrary",)
+        ),
+        name="project_qkv",
+    )(my_frames, tokens_here, mod_first, qkv_weight, qkv_weight, qkv_weight, *tables)
+
+
+def head_stack(values):
+    lane = lax.broadcasted_iota(jnp.int32, values.shape, 1)
+    zero = jnp.zeros_like(values)
+    return jnp.concatenate(
+        [jnp.where(lane < HEAD, values, zero), jnp.where(lane < HEAD, zero, values)], axis=0
+    )
+
+
+def hidden_keys(shape):
+    key_row = lax.broadcasted_iota(jnp.int32, shape, 0)
+    query_column = lax.broadcasted_iota(jnp.int32, shape, 1) % (2 * PATCHES)
+    return (key_row >= PATCHES) & (query_column < PATCHES)
+
+
+def own_heads(values):
+    rows = 2 * PATCHES
+    return jnp.concatenate([values[:HEAD, :rows], values[HEAD:LANES, rows:]], axis=0)
+
+
+def by_frame(frames_ref, source_ref, target_refs):
+    for slot in range(source_ref.shape[0] // PATCHES):
+        rows = pl.ds(pl.multiple_of(frames_ref[slot] * PATCHES, PATCHES), PATCHES)
+        for part, target in enumerate(target_refs):
+            target[rows, :] = source_ref[
+                slot * PATCHES : (slot + 1) * PATCHES, part * LANES : (part + 1) * LANES
+            ]
+
+
+def attend_kernel(
+    frames_ref, slots_ref, qkv_ref, att_ref, ot_ref, lse_ref, q_ref, k_ref, v_ref, vt_ref
+):
+    token_count = qkv_ref.shape[0]
+    by_frame(frames_ref, qkv_ref, (q_ref, k_ref, v_ref))
+    vt_ref[:LANES, :] = v_ref[...].T
+    vt_ref[LANES:, :] = jnp.ones((vt_ref.shape[0] - LANES, token_count), jnp.bfloat16)
+    step = 2 * PATCHES
+    for turn in range(token_count // step):
+        here = slice(turn * step, (turn + 1) * step)
+        queries = head_stack(q_ref[here, :])
+        ranges = [here] if turn == 0 else [slice(0, turn * step), here]
+        raw = [
+            lax.dot_general(k_ref[keys, :], queries, NT, preferred_element_type=jnp.float32)
+            for keys in ranges
+        ]
+        raw[-1] = jnp.where(hidden_keys(raw[-1].shape), NEG_LARGE, raw[-1])
+        top = jnp.max(raw[-1], axis=0, keepdims=True)
+        for part in raw[:-1]:
+            top = jnp.maximum(top, jnp.max(part, axis=0, keepdims=True))
+        top = top * EXP_SCALE
+        summed = None
+        for keys, part in zip(ranges, raw):
+            weights = jnp.exp2(part * EXP_SCALE - top).astype(jnp.bfloat16)
+            update = lax.dot_general(
+                vt_ref[:, keys], weights, NN, preferred_element_type=jnp.float32
+            )
+            summed = update if summed is None else summed + update
+        totals = summed[LANES : LANES + 1, :]
+        lse_ref[turn : turn + 1, :] = top + jnp.log2(totals)
+        out = own_heads(summed[:LANES, :] / totals)
+        ot_ref[:, here] = out
+        rounded = out.T.astype(jnp.bfloat16)
+        for half in range(2):
+            slot = slots_ref[2 * turn + half]
+            rows = pl.ds(pl.multiple_of(slot * PATCHES, PATCHES), PATCHES)
+            att_ref[rows, :] = rounded[half * PATCHES : (half + 1) * PATCHES, :]
+
+
+def attend(frames, slots, qkv):
+    token_count = qkv.shape[0]
+    turns = token_count // (2 * PATCHES)
+    return pl.pallas_call(
+        attend_kernel,
+        in_specs=[
+            pl.BlockSpec(memory_space=pltpu.SMEM),
+            pl.BlockSpec(memory_space=pltpu.SMEM),
+            pl.BlockSpec(memory_space=pltpu.VMEM),
+        ],
+        out_specs=[pl.BlockSpec(memory_space=pltpu.VMEM)] * 3,
+        out_shape=[
+            jax.ShapeDtypeStruct((token_count, LANES), jnp.bfloat16),
+            jax.ShapeDtypeStruct((LANES, token_count), jnp.float32),
+            jax.ShapeDtypeStruct((turns, 4 * PATCHES), jnp.float32),
+        ],
+        scratch_shapes=[pltpu.VMEM((token_count, LANES), jnp.bfloat16)] * 3
+        + [pltpu.VMEM((LANES + 16, token_count), jnp.bfloat16)],
+        compiler_params=pltpu.CompilerParams(vmem_limit_bytes=VMEM_LIMIT),
+        name="attend",
+    )(frames, slots, qkv)
+
+
+def attend_back_kernel(
+    frames_ref,
+    slots_ref,
+    qkv_ref,
+    grad_ref,
+    ot_ref,
+    lse_ref,
+    fcos_ref,
+    fsin_ref,
+    pcos_ref,
+    psin_ref,
+    out_ref,
+    q_ref,
+    k_ref,
+    v_ref,
+    d_ref,
+    kt_ref,
+    dk_ref,
+    dv_ref,
+):
+    token_count = qkv_ref.shape[0]
+    by_frame(frames_ref, qkv_ref, (q_ref, k_ref, v_ref))
+    by_frame(frames_ref, grad_ref, (d_ref,))
+    kt_ref[...] = k_ref[...].T
+    step = 2 * PATCHES
+
+    def put(frame, part, values):
+        rows = pl.ds(pl.multiple_of(slots_ref[frame] * PATCHES, PATCHES), PATCHES)
+        out_ref[rows, part * LANES : (part + 1) * LANES] = values
+
+    def turn_back(frame, values):
+        values = values.astype(jnp.bfloat16).astype(jnp.float32)
+        cosine = pcos_ref[...] + fcos_ref[frame : frame + 1, :]
+        sine = psin_ref[...] + fsin_ref[frame : frame + 1, :]
+        return (values * cosine - partner_lanes(values) * sine).astype(jnp.bfloat16)
+
+    for turn in range(token_count // step):
+        here = slice(turn * step, (turn + 1) * step)
+        queries = head_stack(q_ref[here, :])
+        grads_here = d_ref[here, :]
+        grads = head_stack(grads_here)
+        product = grads_here.astype(jnp.float32).T * ot_ref[:, here]
+        delta = jnp.concatenate(
+            [
+                jnp.sum(product[:HEAD, :], axis=0, keepdims=True),
+                jnp.sum(product[HEAD:, :], axis=0, keepdims=True),
+            ],
+            axis=1,
+        )
+        lse = lse_ref[turn : turn + 1, :]
+        ranges = [here] if turn == 0 else [here, slice(0, turn * step)]
+        total = None
+        for keys in ranges:
+            raw = lax.dot_general(
+                k_ref[keys, :], queries, NT, preferred_element_type=jnp.float32
+            )
+            weights = jnp.exp2(raw * EXP_SCALE - lse)
+            if keys is here:
+                weights = jnp.where(hidden_keys(weights.shape), 0.0, weights)
+            weight_grad = lax.dot_general(
+                v_ref[keys, :], grads, NT, preferred_element_type=jnp.float32
+            )
+            score_grad = (weights * (weight_grad - delta)).astype(jnp.bfloat16)
+            value_part = lax.dot_general(
+                weights.astype(jnp.bfloat16), grads, NN, preferred_element_type=jnp.float32
+            )
+            key_part = lax.dot_general(
+                score_grad, queries, NN, preferred_element_type=jnp.float32
+            )
+            if keys is here:
+                dv_ref[keys, :] = value_part
+                dk_ref[keys, :] = key_part
+            else:
+                dv_ref[keys, :] += value_part
+                dk_ref[keys, :] += key_part
+            update = lax.dot_general(
+                kt_ref[:, keys], score_grad, NN, preferred_element_type=jnp.float32
+            )
+            total = update if total is None else total + update
+        query_grad = own_heads(total).T * SCALE
+        for half in range(2):
+            put(
+                2 * turn + half,
+                0,
+                turn_back(2 * turn + half, query_grad[half * PATCHES : (half + 1) * PATCHES, :]),
+            )
+    for frame in range(token_count // PATCHES):
+        rows = slice(frame * PATCHES, (frame + 1) * PATCHES)
+        put(frame, 1, turn_back(frame, dk_ref[rows, :] * SCALE))
+        put(frame, 2, dv_ref[rows, :].astype(jnp.bfloat16))
+
+
+def attend_back(frames, slots, qkv, grads, ot, lse, tables):
+    token_count = qkv.shape[0]
+    smem = pl.BlockSpec(memory_space=pltpu.SMEM)
+    vmem = pl.BlockSpec(memory_space=pltpu.VMEM)
+    return pl.pallas_call(
+        attend_back_kernel,
+        in_specs=[smem, smem] + [vmem] * 8,
+        out_specs=vmem,
+        out_shape=jax.ShapeDtypeStruct((token_count, 3 * LANES), jnp.bfloat16),
+        scratch_shapes=[pltpu.VMEM((token_count, LANES), jnp.bfloat16)] * 4
+        + [pltpu.VMEM((LANES, token_count), jnp.bfloat16)]
+        + [pltpu.VMEM((token_count, LANES), jnp.float32)] * 2,
+        compiler_params=pltpu.CompilerParams(vmem_limit_bytes=VMEM_LIMIT),
+        name="attend_back",
+    )(frames, slots, qkv, grads, ot, lse, *tables)
+
+
+def swap(values, bit):
+    count = lax.axis_size(AXES)
+    return lax.ppermute(values, AXES, [(index, index ^ bit) for index in range(count)])
+
+
+def gather_pairs(values):
+    bit = 1
+    while bit < lax.axis_size(AXES):
+        values = jnp.concatenate([values, swap(values, bit)], axis=0)
+        bit *= 2
+    return values
+
+
+def halving_sum(values, order):
+    index = lax.axis_index(AXES)
+    left = sorted(order)
+    for position, bit in enumerate(order):
+        place = left.index(bit)
+        above = 2 ** (len(left) - 1 - place)
+        split = values.reshape((above, 2, 2**place) + values.shape[1:])
+        mine = (index >> bit) & 1
+        keep = lax.dynamic_index_in_dim(split, mine, 1, keepdims=False)
+        send = lax.dynamic_index_in_dim(split, 1 - mine, 1, keepdims=False)
+        got = swap(send, 2**bit)
+        total = keep.astype(jnp.float32) + got.astype(jnp.float32)
+        if position < len(order) - 1:
+            total = total.astype(jnp.bfloat16)
+        values = total.reshape((above * 2**place,) + values.shape[1:])
+        left.remove(bit)
+    return values[0]
+
+
+def sum_shares(values):
+    count = lax.axis_size(AXES)
+    rows, columns = values.shape
+    blocks = values.reshape(count, rows // count, columns)
+    bits = list(range(count.bit_length() - 1))
+    other = [0, 2, 1] + bits[3:]
+    half = columns // 2
+    return jnp.concatenate(
+        [halving_sum(blocks[:, :, :half], bits), halving_sum(blocks[:, :, half:], other)], axis=1
+    )
+
+
+def local_heads(
+    tokens,
+    noise_levels,
+    group_map,
+    noise_table,
+    mod_weight,
+    mod_bias,
+    qkv_weight,
+    out_weight,
+    fc1_weight,
+    fc2_weight,
+    out_cotangent,
+):
+    rows_here = 2 * PATCHES
+    frame_count = group_map.shape[0]
+    groups = D // LANES
+    clips = lax.axis_size("clip")
+    device_count = lax.axis_size(AXES)
+    index = lax.axis_index(AXES)
+    slots = jnp.argsort(group_map).astype(jnp.int32)
+    my_frames = lax.dynamic_slice_in_dim(group_map, 2 * lax.axis_index("blk"), 2)
+    tables = rope_tables(frame_count)
+    embedded = jnp.concatenate(
+        [
+            lax.dynamic_slice_in_dim(noise_table, noise_levels[0, my_frames[slot]], 1)
+            for slot in range(2)
+        ]
+    ).astype(jnp.float32)
+    activated = jax.nn.silu(embedded).astype(jnp.bfloat16)
+    modulation = (
+        jnp.dot(activated, mod_weight, preferred_element_type=jnp.float32)
+        + mod_bias.astype(jnp.float32)[None, :]
+    )
+    shift_one, scale_one, gate_one, shift_two, scale_two, gate_two = [
+        modulation[:, member * D : (member + 1) * D][:, None, :] for member in range(6)
+    ]
+    qkv_out, first_in = project_qkv(
+        my_frames, tokens.reshape(rows_here, D), modulation[:, : 2 * D], qkv_weight, tables
+    )
+    qkv_heads = lax.all_to_all(qkv_out, "blk", 0, 0, tiled=True).reshape(-1, 3 * LANES)
+    att_heads, ot, lse = attend(group_map, slots, qkv_heads)
+    attended_low = (
+        lax.all_to_all(att_heads.reshape(groups, rows_here, LANES), "blk", 0, 0, tiled=True)
+        .transpose(1, 0, 2)
+        .reshape(rows_here, D)
+    )
+    inputs_here = tokens[0].astype(jnp.float32)
+    attn_out = jnp.dot(attended_low, out_weight, preferred_element_type=jnp.float32).reshape(
+        2, PATCHES, D
+    )
+    middle = inputs_here + gate_one * attn_out
+    normed_two, inverse_two = normalize(middle)
+    second_in = (
+        (normed_two * (1.0 + scale_two) + shift_two).astype(jnp.bfloat16).reshape(rows_here, D)
+    )
+    up_lin = jnp.dot(second_in, fc1_weight, preferred_element_type=jnp.float32)
+    hidden = jax.nn.gelu(up_lin, approximate=False).astype(jnp.bfloat16)
+    mlp_out = jnp.dot(hidden, fc2_weight, preferred_element_type=jnp.float32).reshape(2, PATCHES, D)
+    layer_out = (middle + gate_two * mlp_out).astype(jnp.bfloat16)[None]
+    cotangent = out_cotangent[0].astype(jnp.float32)
+    d_gate_two = jnp.sum(cotangent * mlp_out, axis=1)
+    d_mlp = (cotangent * gate_two).astype(jnp.bfloat16).reshape(rows_here, D)
+    lower_part = jnp.einsum("rf,rd->fd", hidden, d_mlp, preferred_element_type=jnp.float32)
+    lower_share = sum_shares(lower_part.astype(jnp.bfloat16))
+    d_hidden = jnp.einsum("rd,fd->rf", d_mlp, fc2_weight, preferred_element_type=jnp.float32)
+    unused_value, gelu_pull = jax.vjp(partial(jax.nn.gelu, approximate=False), up_lin)
+    d_up = gelu_pull(d_hidden)[0].astype(jnp.bfloat16)
+    upper_part = jnp.einsum("rc,rf->cf", second_in, d_up, preferred_element_type=jnp.float32)
+    upper_share = sum_shares(upper_part.astype(jnp.bfloat16))
+    d_second = jnp.einsum(
+        "rf,cf->rc", d_up, fc1_weight, preferred_element_type=jnp.float32
+    ).reshape(2, PATCHES, D)
+    d_shift_two = jnp.sum(d_second, axis=1)
+    d_scale_two = jnp.sum(d_second * normed_two, axis=1)
+    d_middle = cotangent + norm_backward(d_second * (1.0 + scale_two), normed_two, inverse_two)
+    d_gate_one = jnp.sum(d_middle * attn_out, axis=1)
+    d_attn = (d_middle * gate_one).astype(jnp.bfloat16).reshape(rows_here, D)
+    outw_part = jnp.einsum("rc,rd->cd", attended_low, d_attn, preferred_element_type=jnp.float32)
+    outw_share = sum_shares(outw_part.astype(jnp.bfloat16))
+    d_attended = jnp.einsum(
+        "rd,cd->rc", d_attn, out_weight, preferred_element_type=jnp.float32
+    ).astype(jnp.bfloat16)
+    early_all = gather_pairs(
+        jnp.concatenate([d_gate_one, d_shift_two, d_scale_two, d_gate_two], axis=1).astype(
+            jnp.bfloat16
+        )[None]
+    )
+    grad_heads = lax.all_to_all(
+        d_attended.reshape(rows_here, groups, LANES).transpose(1, 0, 2), "blk", 0, 0, tiled=True
+    ).reshape(-1, LANES)
+    d_heads = attend_back(group_map, slots, qkv_heads, grad_heads, ot, lse, tables)
+    d_qkv = (
+        lax.all_to_all(d_heads.reshape(groups, rows_here, 3 * LANES), "blk", 0, 0, tiled=True)
+        .reshape(groups, rows_here, 3, LANES)
+        .transpose(1, 2, 0, 3)
+        .reshape(rows_here, 3 * D)
+    )
+    qkv_part = jnp.einsum("rc,rk->ck", first_in, d_qkv, preferred_element_type=jnp.float32)
+    qkv_share = sum_shares(qkv_part.astype(jnp.bfloat16))
+    d_first = jnp.einsum(
+        "rk,ck->rc", d_qkv, qkv_weight, preferred_element_type=jnp.float32
+    ).reshape(2, PATCHES, D)
+    normed_one, inverse_one = normalize(inputs_here)
+    d_shift_one = jnp.sum(d_first, axis=1)
+    d_scale_one = jnp.sum(d_first * normed_one, axis=1)
+    tokens_grad = (
+        d_middle + norm_backward(d_first * (1.0 + scale_one), normed_one, inverse_one)
+    ).astype(jnp.bfloat16)[None]
+    late_all = gather_pairs(
+        jnp.concatenate([d_shift_one, d_scale_one], axis=1).astype(jnp.bfloat16)[None]
+    )
+    d_mod_all = jnp.concatenate([late_all, early_all], axis=2).reshape(2 * device_count, 6 * D)
+    member_index = index ^ jnp.arange(device_count, dtype=jnp.int32)
+    levels_all = gather_pairs(
+        lax.dynamic_slice_in_dim(
+            jnp.broadcast_to(noise_levels[0][my_frames][:, None], (2, LANES)), 0, 2
+        )[None]
+    )[:, :, 0].reshape(2 * device_count)
+    share = D // device_count
+    level_hot = jnp.arange(LEVELS, dtype=jnp.int32)[:, None] == levels_all[None, :]
+    table_columns = lax.dynamic_slice_in_dim(noise_table, index * share, share, 1)
+    embedded_columns = jnp.einsum(
+        "ls,lc->sc",
+        level_hot.astype(jnp.bfloat16),
+        table_columns,
+        preferred_element_type=jnp.float32,
+    )
+    activated_columns, silu_pull = jax.vjp(jax.nn.silu, embedded_columns)
+    modw_share = jnp.einsum(
+        "sc,sk->ck",
+        activated_columns.astype(jnp.bfloat16),
+        d_mod_all,
+        preferred_element_type=jnp.float32,
+    )
+    weight_rows = lax.dynamic_slice_in_dim(mod_weight, index * share, share, 0)
+    d_activated = jnp.einsum("sk,ck->sc", d_mod_all, weight_rows, preferred_element_type=jnp.float32)
+    d_embedded = silu_pull(d_activated)[0]
+    table_share = jnp.dot(
+        level_hot.astype(jnp.float32), d_embedded, precision=lax.Precision.HIGHEST
+    )
+    bias_columns = 6 * D // device_count
+    bias_share = jnp.sum(
+        lax.dynamic_slice_in_dim(d_mod_all, index * bias_columns, bias_columns, 1).astype(
+            jnp.float32
+        ),
+        axis=0,
+    )
+    return (
+        layer_out,
+        tokens_grad,
+        table_share,
+        modw_share,
+        bias_share,
+        qkv_share,
+        outw_share,
+        upper_share,
+        lower_share,
+    )
+
+
 def solution(mesh):
+    pair_split = mesh.shape["blk"] * LANES == D
     return jax.shard_map(
-        local,
+        local_heads if pair_split else local,
         mesh=mesh,
         in_specs=(
             P("clip", "blk", None, None),

time: 1280 us -> 496 us (0.39)
  waiting for transfers between devices: 664 us -> 208 us
  matrix products: 245 us -> 62.9 us
  blocking collectives: 180 us -> 0 us
  starting transfers between devices: 1.07 us -> 73.9 us
  other arithmetic: 85.5 us -> 42.3 us
  Pallas kernels: 0 us -> 35.6 us
  loops' own time: 17.1 us -> 0 us
    reduce_scatter x5 -> x0, waiting for transfers between devices: 521 us -> none  [the longest x1 187 us: local(): lax.psum_scatter(lower_part, ('blk', 'clip'), scatter_dimension=0, tiled=...]
    dot_general x45 -> x16, matrix products: 245 us -> 62.9 us  [the longest x1 13.3 us: local_heads(): jnp.einsum('rd,fd->rf', d_mlp, fc2_weight, preferred_element_type=jnp.flo...]
    ppermute x0 -> x55, waiting for transfers between devices: none -> 179 us  [swap(): lax.ppermute(values, AXES, [(index, index ^ bit) for index in range(count)])]
    all_gather x4 -> x0, waiting for transfers between devices: 142 us -> none  [the longest x1 75.8 us: local(): values_piece = lax.all_gather(value_part, 'blk', axis=0, tiled=True)]
    all_gather x4 -> x0, blocking collectives: 142 us -> none  [the longest x1 41.9 us: local(): lax.all_gather(d_mod_low, ('blk', 'clip'), axis=0, tiled=True)]
    ppermute x0 -> x55, starting transfers between devices: none -> 53.3 us  [swap(): lax.ppermute(values, AXES, [(index, index ^ bit) for index in range(count)])]
    unnamed x1 -> x0, blocking collectives: 37.5 us -> none
    pallas_call x0 -> x3, Pallas kernels: none -> 35.6 us  [the longest x1 15.3 us: attend_back(): pl.pallas_call(attend_back_kernel, in_specs=[smem, smem] + [vmem] * 8, ou...]
  transfers between devices with their start and end apart: 9 -> 59, of which waited for: 5 -> 36; matrix products, arithmetic and copies ran while one was open for 28% -> 19% of each run, Pallas kernels for 0% -> 5%
where the time goes in v1:
time: 496 us; the launch traced here: 487 us
  waiting for transfers between devices  208 us (42%)
  starting transfers between devices  73.9 us (15%)
  matrix products  62.9 us (13%)
  local copies, waits for them, and re-layouts  53.3 us (11%)
  other arithmetic  42.3 us (9%)
  Pallas kernels  35.6 us (7%)
  between operations  10.3 us (2%)
    ppermute x55, waiting for transfers between devices, swap(): lax.ppermute(values, AXES, [(index, index ^ bit) for index in range(count)])  179 us
    ppermute x55, starting transfers between devices, swap(): lax.ppermute(values, AXES, [(index, index ^ bit) for index in range(count)])  53.3 us
    all_to_all x1, waiting for transfers between devices, local_heads(): lax.all_to_all(qkv_out, 'blk', 0, 0, tiled=True).reshape(-1, 3 * LANES)  29.5 us
    convert_element_type x32, other arithmetic, halving_sum(): total = total.astype(jnp.bfloat16)  26 us
    squeeze x40, local copies, waits for them, and re-layouts, halving_sum(): send = lax.dynamic_index_in_dim(split, 1 - mine, 1, keepdims=False)  15.7 us
    pallas_call x1, Pallas kernels, attend_back(): pl.pallas_call(attend_back_kernel, in_specs=[smem, smem] + [vmem] * 8, ou...  15.3 us
    slice x4, local copies, waits for them, and re-layouts, sum_shares(): blocks[:, :, :half]  15.2 us
    dot_general x1, matrix products, local_heads(): jnp.einsum('rd,fd->rf', d_mlp, fc2_weight, preferred_element_type=jnp.flo...  13.3 us
  transfers between devices with their start and end apart: 59, of which 36 were waited for; matrix products, arithmetic and copies ran while one was open for 19% of the time, Pallas kernels for 5%

profile of v1, /device:TPU:0, one launch (start us, length us, event | category | flops | bytes accessed | tf_op | source)
XLA Modules:
  0.0 486.6 jit_solution(6855258162220398210)
XLA Ops:
  12.9 6.3 %convolution_add_fusion = f32[2,6144]{1,0:T(2,128)S(1)} fusion(bf16[1024,6144]{1,0:T(8,128)(2,1)} %param.15, f32[6144]{0:T(1024)S(1)} %convert_element_type.731, bf16[1,1024]{1,0:T(2,128)(2,1)S(1)} %get-tuple-element.45, bf16[1,1024]{1,0:T(2,128)(2,1)S(1)} %get-tuple-element.44), kind=kOutput, calls=%fused_computation.3 | convolution fusion | flops 25196544 | bytes 12660736 | tf_op jit(solution)/shard_map/dot_general | solution.py:751
  21.5 10.0 %project_qkv.1 = (bf16[8,256,384]{2,1,0:T(8,128)(2,1)}, bf16[256,1024]{1,0:T(8,128)(2,1)}) custom-call(s32[2]{0:T(128)} %copy-done.41, bf16[256,1024]{1,0:T(8,128)(2,1)} %bitcast.385, f32[2,2048]{1,0:T(2,128)} %slice.71.mod_ref, bf16[1024,3072]{1,0:T(8,128)(2,1)} %vw_ref.1, bf16[1024,3072]{1,0:T(8,128)(2,1)} %vw_ref.1, bf16[1024,3072]{1,0:T(8,128)(2,1)} %vw_ref.1, ...), custom_call_target="tpu_custom_call" | custom-call | tf_op jit(solution)/shard_map/project_qkv/pallas_call | solution.py:454
  31.5 7.4 %all-to-all-start = ((bf16[8,256,384]{2,1,0:T(8,128)(2,1)}), bf16[8,256,384]{2,1,0:T(8,128)(2,1)}, u32[]{:S(2)}, u32[]{:S(2)}) async-start(bf16[8,256,384]{2,1,0:T(8,128)(2,1)} %get-tuple-element.16), calls=%async_computation | async-start | bytes 3145728 | tf_op jit(solution)/shard_map/all_to_all | solution.py:760
  46.5 29.5 %all-to-all-done = bf16[8,256,384]{2,1,0:T(8,128)(2,1)} async-done(((bf16[8,256,384]{2,1,0:T(8,128)(2,1)}), bf16[8,256,384]{2,1,0:T(8,128)(2,1)}, u32[]{:S(2)}, u32[]{:S(2)}) %all-to-all-start) | async-done | bytes 1572896 | tf_op jit(solution)/shard_map/all_to_all | solution.py:760
  76.1 10.3 %attend.1 = (bf16[2048,128]{1,0:T(8,128)(2,1)}, f32[128,2048]{1,0:T(8,128)}, f32[8,512]{1,0:T(8,128)}) custom-call(s32[16]{0:T(128)} %frames_ref.3, s32[16]{0:T(128)} %get-tuple-element.15.slots_ref, bf16[2048,384]{1,0:T(8,128)(2,1)} %bitcast.6.qkv_ref), custom_call_target="tpu_custom_call" | custom-call | tf_op jit(solution)/shard_map/attend/pallas_call | solution.py:548
  94.4 6.6 %collective-permute-done.3 = s32[8,2,128]{2,0,1:T(8,128)S(1)} collective-permute-done((s32[8,2,128]{2,0,1:T(8,128)S(1)}, s32[8,2,128]{2,0,1:T(8,128)S(1)}, u32[]{:S(2)}, u32[]{:S(2)}) %collective-permute-start.3) | collective-permute-done | bytes 8224 | tf_op jit(solution)/shard_map/ppermute | solution.py:679
  113.8 5.9 %fusion.97 = f32[256,4096]{1,0:T(8,128)S(1)} fusion(bf16[256,1024]{1,0:T(8,128)(2,1)S(1)} %bitcast.418, bf16[1024,4096]{1,0:T(8,128)(2,1)} %param.19), kind=kOutput, calls=%fused_computation.292 | convolution fusion | flops 2147483648 | bytes 13107200 | tf_op jit(solution)/shard_map/dot_general | solution.py:776
  119.7 13.3 %add_convert_fusion = (bf16[256,4096]{1,0:T(8,128)(2,1)S(1)}, f32[256,4096]{1,0:T(8,128)S(1)}) fusion(f32[256,4096]{1,0:T(8,128)S(1)} %fusion.97, bf16[256,1024]{1,0:T(8,128)(2,1)S(1)} %copy-done.26, bf16[4096,1024]{1,0:T(8,128)(2,1)S(1)} %bitcast.465), kind=kOutput, calls=%fused_computation.17 | convolution fusion | flops 2222981120 | bytes 19398656 | tf_op jit(solution)/shard_map/rd,fd->rf/dot_general | solution.py:785
  135.5 5.7 %convolution_convert_fusion.1 = bf16[1024,4096]{1,0:T(8,128)(2,1)} fusion(bf16[256,1024]{1,0:T(8,128)(2,1)S(1)} %bitcast.419, bf16[256,4096]{1,0:T(8,128)(2,1)S(1)} %get-tuple-element.32), kind=kOutput, calls=%fused_computation.2 | convolution fusion | flops 2151677952 | bytes 11010048 | tf_op jit(solution)/shard_map/rc,rf->cf/dot_general | solution.py:788
  141.9 5.7 %fusion.98 = f32[256,1024]{1,0:T(8,128)S(1)} fusion(bf16[256,4096]{1,0:T(8,128)(2,1)S(1)} %multiply_convert_fusion, bf16[4096,1024]{1,0:T(8,128)(2,1)} %param.20), kind=kOutput, calls=%fused_computation.293 | convolution fusion | flops 2147483648 | bytes 11534336 | tf_op jit(solution)/shard_map/dot_general | solution.py:778
  147.7 5.7 %convolution_convert_fusion = bf16[4096,1024]{1,0:T(8,128)(2,1)} fusion(bf16[256,4096]{1,0:T(8,128)(2,1)S(1)} %multiply_convert_fusion, bf16[256,1024]{1,0:T(8,128)(2,1)S(1)} %copy-done.26), kind=kOutput, calls=%fused_computation.1 | convolution fusion | flops 2151677952 | bytes 11010048 | tf_op jit(solution)/shard_map/rf,rd->fd/dot_general | solution.py:783
  175.4 9.9 %fusion.92 = (bf16[32,128,512]{2,1,0:T(8,128)(2,1)S(1)}, bf16[32,128,512]{2,1,0:T(8,128)(2,1)S(1)}) fusion(bf16[32,128,1024]{2,1,0:T(8,128)(2,1)S(1)} %bitcast.356), kind=kLoop, calls=%fused_computation.287 | loop fusion | bytes 16777216 | tf_op jit(solution)/shard_map/slice | solution.py:717
  205.1 6.1 %collective-permute-done.14 = bf16[16,2,4096]{2,1,0:T(2,128)(2,1)S(1)} collective-permute-done((bf16[16,2,4096]{2,1,0:T(2,128)(2,1)S(1)}, bf16[16,2,4096]{2,1,0:T(2,128)(2,1)S(1)}, u32[]{:S(2)}, u32[]{:S(2)}) %collective-permute-start.14) | collective-permute-done | bytes 262176 | tf_op jit(solution)/shard_map/ppermute | solution.py:679
  214.0 6.5 %collective-permute-done.26 = bf16[8,1,32,512]{3,2,0,1:T(8,128)(2,1)S(1)} collective-permute-done((bf16[8,1,32,512]{3,2,0,1:T(8,128)(2,1)S(1)}, bf16[8,1,32,512]{3,2,0,1:T(8,128)(2,1)S(1)}, u32[]{:S(2)}, u32[]{:S(2)}) %collective-permute-start.26) | collective-permute-done | bytes 262176 | tf_op jit(solution)/shard_map/ppermute | solution.py:679
  222.4 5.5 %collective-permute-done.31 = bf16[4,2,32,512]{3,2,1,0:T(8,128)(2,1)S(1)} collective-permute-done((bf16[4,2,32,512]{3,2,1,0:T(8,128)(2,1)S(1)}, bf16[4,2,32,512]{3,2,1,0:T(8,128)(2,1)S(1)}, u32[]{:S(2)}, u32[]{:S(2)}) %collective-permute-start.31) | collective-permute-done | bytes 262176 | tf_op jit(solution)/shard_map/ppermute | solution.py:679
  229.8 15.3 %attend_back.1 = bf16[2048,384]{1,0:T(8,128)(2,1)} custom-call(s32[16]{0:T(128)} %frames_ref.3, s32[16]{0:T(128)} %get-tuple-element.15.slots_ref, bf16[2048,384]{1,0:T(8,128)(2,1)} %bitcast.6.qkv_ref, bf16[2048,128]{1,0:T(8,128)(2,1)} %bitcast.21.grad_ref, f32[128,2048]{1,0:T(8,128)} %get-tuple-element.18.ot_ref, f32[8,512]{1,0:T(8,128)} %get-tuple-element.19.lse_ref, ...), custom_call_target="tpu_custom_call" | custom-call | tf_op jit(solution)/shard_map/attend_back/pallas_call | solution.py:664
  259.3 18.3 %collective-permute-done.28 = bf16[2,1,32,512]{3,2,0,1:T(8,128)(2,1)S(1)} collective-permute-done((bf16[2,1,32,512]{3,2,0,1:T(8,128)(2,1)S(1)}, bf16[2,1,32,512]{3,2,0,1:T(8,128)(2,1)S(1)}, u32[]{:S(2)}, u32[]{:S(2)}) %collective-permute-start.28) | collective-permute-done | bytes 65568 | tf_op jit(solution)/shard_map/ppermute | solution.py:679
  280.1 7.9 %collective-permute-done.33 = bf16[2,1,32,512]{3,2,1,0:T(8,128)(2,1)S(1)} collective-permute-done((bf16[2,1,32,512]{3,2,1,0:T(8,128)(2,1)S(1)}, bf16[2,1,32,512]{3,2,1,0:T(8,128)(2,1)S(1)}, u32[]{:S(2)}, u32[]{:S(2)}) %collective-permute-start.33) | collective-permute-done | bytes 65568 | tf_op jit(solution)/shard_map/ppermute | solution.py:679
  313.6 14.4 %collective-permute-done.36 = bf16[8,1,32,2048]{3,2,0,1:T(8,128)(2,1)S(1)} collective-permute-done((bf16[8,1,32,2048]{3,2,0,1:T(8,128)(2,1)S(1)}, bf16[8,1,32,2048]{3,2,0,1:T(8,128)(2,1)S(1)}, u32[]{:S(2)}, u32[]{:S(2)}) %collective-permute-start.36) | collective-permute-done | bytes 1048608 | tf_op jit(solution)/shard_map/ppermute | solution.py:679
  334.2 16.3 %collective-permute-done.46 = bf16[8,1,128,512]{3,2,0,1:T(8,128)(2,1)S(1)} collective-permute-done((bf16[8,1,128,512]{3,2,0,1:T(8,128)(2,1)S(1)}, bf16[8,1,128,512]{3,2,0,1:T(8,128)(2,1)S(1)}, u32[]{:S(2)}, u32[]{:S(2)}) %collective-permute-start.46) | collective-permute-done | bytes 1048608 | tf_op jit(solution)/shard_map/ppermute | solution.py:679
  364.1 5.6 %fusion.35 = (bf16[2,1024]{1,0:T(2,128)(2,1)S(1)}, f32[2,128]{1,0:T(2,128)S(1)}, f32[2,128]{1,0:T(2,128)S(1)}, bf16[2,1024]{1,0:T(2,128)(2,1)S(1)}, f32[2,128,1024]{2,1,0:T(8,128)S(1)}) fusion(bf16[1,2,128,1024]{3,2,1,0:T(8,128)(2,1)S(1)} %copy-done.15, f32[2,128]{1,0:T(2,128)S(1)} %add_rsqrt_fusion, f32[2,128]{1,0:T(2,128)S(1)} %broadcast_multiply_fusion.2, ...), kind=kOutput, calls=%fused_computation.73 | convolution fusion | flops 1613229568 | bytes 9457664 | tf_op jit(solution)/shard_map/rk,ck->rc/dot_general | solution.py:820
  422.0 5.7 %collective-permute-done.39 = bf16[1,1,32,2048]{3,2,0,1:T(8,128)(2,1)S(1)} collective-permute-done((bf16[1,1,32,2048]{3,2,0,1:T(8,128)(2,1)S(1)}, bf16[1,1,32,2048]{3,2,0,1:T(8,128)(2,1)S(1)}, u32[]{:S(2)}, u32[]{:S(2)}) %collective-permute-start.39) | collective-permute-done | bytes 131104 | tf_op jit(solution)/shard_map/ppermute | solution.py:679
  444.1 12.8 %collective-permute-done.16 = bf16[8,1,32,1536]{3,2,0,1:T(8,128)(2,1)S(1)} collective-permute-done((bf16[8,1,32,1536]{3,2,0,1:T(8,128)(2,1)S(1)}, bf16[8,1,32,1536]{3,2,0,1:T(8,128)(2,1)S(1)}, u32[]{:S(2)}, u32[]{:S(2)}) %collective-permute-start.16) | collective-permute-done | bytes 786464 | tf_op jit(solution)/shard_map/ppermute | solution.py:679
  462.8 5.5 %collective-permute-done.17 = bf16[4,1,32,1536]{3,2,0,1:T(8,128)(2,1)S(1)} collective-permute-done((bf16[4,1,32,1536]{3,2,0,1:T(8,128)(2,1)S(1)}, bf16[4,1,32,1536]{3,2,0,1:T(8,128)(2,1)S(1)}, u32[]{:S(2)}, u32[]{:S(2)}) %collective-permute-start.17) | collective-permute-done | bytes 393248 | tf_op jit(solution)/shard_map/ppermute | solution.py:679
  (381 shorter events, 239.9 us)
Async XLA Ops:
  31.5 44.5 %all-to-all-start = ((bf16[8,256,384]{2,1,0:T(8,128)(2,1)}), bf16[8,256,384]{2,1,0:T(8,128)(2,1)}, u32[]{:S(2)}, u32[]{:S(2)}) async-start(bf16[8,256,384]{2,1,0:T(8,128)(2,1)} %get-tuple-element.16), calls=%async_computation | async-start | bytes 3145728 | tf_op jit(solution)/shard_map/all_to_all | solution.py:760
  44.4 47.8 %collective-permute-start.2 = (s32[4,2,128]{2,0,1:T(4,128)S(1)}, s32[4,2,128]{2,0,1:T(4,128)S(1)}, u32[]{:S(2)}, u32[]{:S(2)}) collective-permute-start(s32[4,2,128]{2,0,1:T(4,128)S(1)} %pad_add_fusion.1), channel_id=1, source_target_pairs={{0,4},{1,5},{2,6},{3,7},{4,0},{5,1},{6,2},{7,3},{8,12},{9,13},{10,... | collective-permute-start | bytes 12296 | tf_op jit(solution)/shard_map/ppermute | solution.py:679
  158.0 71.8 %all-to-all-start.2 = ((bf16[8,256,128]{2,1,0:T(8,128)(2,1)}), bf16[8,256,128]{2,1,0:T(8,128)(2,1)}, u32[]{:S(2)}, u32[]{:S(2)}) async-start(bf16[8,256,128]{2,1,0:T(8,128)(2,1)} %bitcast.351), calls=%async_computation.2 | async-start | bytes 1048576 | tf_op jit(solution)/shard_map/all_to_all | solution.py:808
  162.9 22.4 %collective-permute-start.10 = (bf16[1,2,4096]{2,1,0:T(2,128)(2,1)S(1)}, bf16[1,2,4096]{2,1,0:T(2,128)(2,1)S(1)}, u32[]{:S(2)}, u32[]{:S(2)}) collective-permute-start(bf16[1,2,4096]{2,1,0:T(2,128)(2,1)S(1)} %get-tuple-element.70), channel_id=1, source_target_pairs={{0,1},{1,0},{2,3},{3,2},{4,5},{5,4},{6,7},{7,6},{8,9},{9,8},{10,11... | collective-permute-start | bytes 49160 | tf_op jit(solution)/shard_map/ppermute | solution.py:679
  165.2 46.3 %collective-permute-start.25 = (bf16[16,1,32,512]{3,2,0,1:T(8,128)(2,1)S(1)}, bf16[16,1,32,512]{3,2,0,1:T(8,128)(2,1)S(1)}, u32[]{:S(2)}, u32[]{:S(2)}) collective-permute-start(bf16[16,1,32,512]{3,2,0,1:T(8,128)(2,1)S(1)} %dynamic-slice_bitcast_fusion.15), channel_id=1, source_target_pairs={{0,1},{1,0},{2,3},{3,2},{4,5},{5,4},{6,7},{7,6},{8,9},{9,8},{10,11... | collective-permute-start | bytes 1572872 | tf_op jit(solution)/shard_map/ppermute | solution.py:679
  165.8 46.5 %collective-permute-start.30 = (bf16[16,1,32,512]{3,2,0,1:T(8,128)(2,1)S(1)}, bf16[16,1,32,512]{3,2,0,1:T(8,128)(2,1)S(1)}, u32[]{:S(2)}, u32[]{:S(2)}) collective-permute-start(bf16[16,1,32,512]{3,2,0,1:T(8,128)(2,1)S(1)} %dynamic-slice_bitcast_fusion.14), channel_id=1, source_target_pairs={{0,1},{1,0},{2,3},{3,2},{4,5},{5,4},{6,7},{7,6},{8,9},{9,8},{10,11... | collective-permute-start | bytes 1572872 | tf_op jit(solution)/shard_map/ppermute | solution.py:679
  174.8 123.7 %collective-permute-start.35 = (bf16[16,1,32,2048]{3,2,0,1:T(8,128)(2,1)}, bf16[16,1,32,2048]{3,2,0,1:T(8,128)(2,1)}, u32[]{:S(2)}, u32[]{:S(2)}) collective-permute-start(bf16[16,1,32,2048]{3,2,0,1:T(8,128)(2,1)} %dynamic-slice_bitcast_fusion.3), channel_id=1, source_target_pairs={{0,1},{1,0},{2,3},{3,2},{4,5},{5,4},{6,7},{7,6},{8,9},{9,8},{10,11... | collective-permute-start | bytes 6291464 | tf_op jit(solution)/shard_map/ppermute | solution.py:679
  175.3 128.2 %collective-permute-start.40 = (bf16[16,1,32,2048]{3,2,0,1:T(8,128)(2,1)}, bf16[16,1,32,2048]{3,2,0,1:T(8,128)(2,1)}, u32[]{:S(2)}, u32[]{:S(2)}) collective-permute-start(bf16[16,1,32,2048]{3,2,0,1:T(8,128)(2,1)} %dynamic-slice_bitcast_fusion.2), channel_id=1, source_target_pairs={{0,1},{1,0},{2,3},{3,2},{4,5},{5,4},{6,7},{7,6},{8,9},{9,8},{10,11... | collective-permute-start | bytes 6291464 | tf_op jit(solution)/shard_map/ppermute | solution.py:679
  211.2 94.8 %collective-permute-start.45 = (bf16[16,1,128,512]{3,2,0,1:T(8,128)(2,1)}, bf16[16,1,128,512]{3,2,0,1:T(8,128)(2,1)}, u32[]{:S(2)}, u32[]{:S(2)}) collective-permute-start(bf16[16,1,128,512]{3,2,0,1:T(8,128)(2,1)} %dynamic-slice_bitcast_fusion.1), channel_id=1, source_target_pairs={{0,1},{1,0},{2,3},{3,2},{4,5},{5,4},{6,7},{7,6},{8,9},{9,8},{10,11... | collective-permute-start | bytes 6291464 | tf_op jit(solution)/shard_map/ppermute | solution.py:679
  211.5 97.9 %collective-permute-start.50 = (bf16[16,1,128,512]{3,2,0,1:T(8,128)(2,1)}, bf16[16,1,128,512]{3,2,0,1:T(8,128)(2,1)}, u32[]{:S(2)}, u32[]{:S(2)}) collective-permute-start(bf16[16,1,128,512]{3,2,0,1:T(8,128)(2,1)} %dynamic-slice_bitcast_fusion), channel_id=1, source_target_pairs={{0,1},{1,0},{2,3},{3,2},{4,5},{5,4},{6,7},{7,6},{8,9},{9,8},{10,11... | collective-permute-start | bytes 6291464 | tf_op jit(solution)/shard_map/ppermute | solution.py:679
  227.9 24.3 %collective-permute-start.27 = (bf16[4,1,32,512]{3,2,0,1:T(8,128)(2,1)S(1)}, bf16[4,1,32,512]{3,2,0,1:T(8,128)(2,1)S(1)}, u32[]{:S(2)}, u32[]{:S(2)}) collective-permute-start(bf16[4,1,32,512]{3,2,0,1:T(8,128)(2,1)S(1)} %dynamic-slice_bitcast_fusion.25), channel_id=1, source_target_pairs={{0,4},{1,5},{2,6},{3,7},{4,0},{5,1},{6,2},{7,3},{8,12},{9,13},{10,... | collective-permute-start | bytes 393224 | tf_op jit(solution)/shard_map/ppermute | solution.py:679
  247.7 109.2 %all-to-all-start.3 = ((bf16[8,256,384]{1,2,0:T(8,128)(2,1)}), bf16[8,256,384]{1,2,0:T(8,128)(2,1)S(1)}, u32[]{:S(2)}, u32[]{:S(2)}) async-start(bf16[8,256,384]{1,2,0:T(8,128)(2,1)} %copy.88), calls=%async_computation.3 | async-start | bytes 3145728 | tf_op jit(solution)/shard_map/all_to_all | solution.py:813
  301.9 26.2 %collective-permute-start.36 = (bf16[8,1,32,2048]{3,2,0,1:T(8,128)(2,1)S(1)}, bf16[8,1,32,2048]{3,2,0,1:T(8,128)(2,1)S(1)}, u32[]{:S(2)}, u32[]{:S(2)}) collective-permute-start(bf16[8,1,32,2048]{3,2,0,1:T(8,128)(2,1)S(1)} %dynamic-slice_bitcast_fusion.9), channel_id=1, source_target_pairs={{0,2},{1,3},{2,0},{3,1},{4,6},{5,7},{6,4},{7,5},{8,10},{9,11},{10,... | collective-permute-start | bytes 3145736 | tf_op jit(solution)/shard_map/ppermute | solution.py:679
  306.0 26.2 %collective-permute-start.41 = (bf16[4,2,32,2048]{3,2,1,0:T(8,128)(2,1)S(1)}, bf16[4,2,32,2048]{3,2,1,0:T(8,128)(2,1)S(1)}, u32[]{:S(2)}, u32[]{:S(2)}) collective-permute-start(bf16[4,2,32,2048]{3,2,1,0:T(8,128)(2,1)S(1)} %dynamic-slice_bitcast_fusion.8), channel_id=1, source_target_pairs={{0,4},{1,5},{2,6},{3,7},{4,0},{5,1},{6,2},{7,3},{8,12},{9,13},{10,... | collective-permute-start | bytes 3145736 | tf_op jit(solution)/shard_map/ppermute | solution.py:679
  308.6 41.9 %collective-permute-start.46 = (bf16[8,1,128,512]{3,2,0,1:T(8,128)(2,1)S(1)}, bf16[8,1,128,512]{3,2,0,1:T(8,128)(2,1)S(1)}, u32[]{:S(2)}, u32[]{:S(2)}) collective-permute-start(bf16[8,1,128,512]{3,2,0,1:T(8,128)(2,1)S(1)} %dynamic-slice_bitcast_fusion.7), channel_id=1, source_target_pairs={{0,2},{1,3},{2,0},{3,1},{4,6},{5,7},{6,4},{7,5},{8,10},{9,11},{10,... | collective-permute-start | bytes 3145736 | tf_op jit(solution)/shard_map/ppermute | solution.py:679
  311.7 42.9 %collective-permute-start.51 = (bf16[4,2,128,512]{3,2,1,0:T(8,128)(2,1)S(1)}, bf16[4,2,128,512]{3,2,1,0:T(8,128)(2,1)S(1)}, u32[]{:S(2)}, u32[]{:S(2)}) collective-permute-start(bf16[4,2,128,512]{3,2,1,0:T(8,128)(2,1)S(1)} %dynamic-slice_bitcast_fusion.6), channel_id=1, source_target_pairs={{0,4},{1,5},{2,6},{3,7},{4,0},{5,1},{6,2},{7,3},{8,12},{9,13},{10,... | collective-permute-start | bytes 3145736 | tf_op jit(solution)/shard_map/ppermute | solution.py:679
  329.4 45.9 %collective-permute-start.37 = (bf16[4,1,32,2048]{3,2,0,1:T(8,128)(2,1)}, bf16[4,1,32,2048]{3,2,0,1:T(8,128)(2,1)}, u32[]{:S(2)}, u32[]{:S(2)}) collective-permute-start(bf16[4,1,32,2048]{3,2,0,1:T(8,128)(2,1)} %dynamic-slice_bitcast_fusion.13), channel_id=1, source_target_pairs={{0,4},{1,5},{2,6},{3,7},{4,0},{5,1},{6,2},{7,3},{8,12},{9,13},{10,... | collective-permute-start | bytes 1572872 | tf_op jit(solution)/shard_map/ppermute | solution.py:679
  333.5 44.9 %collective-permute-start.42 = (bf16[4,1,32,2048]{3,2,1,0:T(8,128)(2,1)}, bf16[4,1,32,2048]{3,2,1,0:T(8,128)(2,1)}, u32[]{:S(2)}, u32[]{:S(2)}) collective-permute-start(bf16[4,1,32,2048]{3,2,1,0:T(8,128)(2,1)} %constant_dynamic-slice_fusion.4), channel_id=1, source_target_pairs={{0,2},{1,3},{2,0},{3,1},{4,6},{5,7},{6,4},{7,5},{8,10},{9,11},{10,... | collective-permute-start | bytes 1572872 | tf_op jit(solution)/shard_map/ppermute | solution.py:679
  351.8 28.8 %collective-permute-start.47 = (bf16[4,1,128,512]{3,2,0,1:T(8,128)(2,1)}, bf16[4,1,128,512]{3,2,0,1:T(8,128)(2,1)}, u32[]{:S(2)}, u32[]{:S(2)}) collective-permute-start(bf16[4,1,128,512]{3,2,0,1:T(8,128)(2,1)} %dynamic-slice_bitcast_fusion.12), channel_id=1, source_target_pairs={{0,4},{1,5},{2,6},{3,7},{4,0},{5,1},{6,2},{7,3},{8,12},{9,13},{10,... | collective-permute-start | bytes 1572872 | tf_op jit(solution)/shard_map/ppermute | solution.py:679
  356.1 27.0 %collective-permute-start.52 = (bf16[4,1,128,512]{3,2,1,0:T(8,128)(2,1)}, bf16[4,1,128,512]{3,2,1,0:T(8,128)(2,1)}, u32[]{:S(2)}, u32[]{:S(2)}) collective-permute-start(bf16[4,1,128,512]{3,2,1,0:T(8,128)(2,1)} %constant_dynamic-slice_fusion.1), channel_id=1, source_target_pairs={{0,2},{1,3},{2,0},{3,1},{4,6},{5,7},{6,4},{7,5},{8,10},{9,11},{10,... | collective-permute-start | bytes 1572872 | tf_op jit(solution)/shard_map/ppermute | solution.py:679
  375.3 61.5 %collective-permute-start.15 = (bf16[16,1,32,1536]{3,2,0,1:T(8,128)(2,1)}, bf16[16,1,32,1536]{3,2,0,1:T(8,128)(2,1)}, u32[]{:S(2)}, u32[]{:S(2)}) collective-permute-start(bf16[16,1,32,1536]{3,2,0,1:T(8,128)(2,1)} %dynamic-slice_bitcast_fusion.5), channel_id=1, source_target_pairs={{0,1},{1,0},{2,3},{3,2},{4,5},{5,4},{6,7},{7,6},{8,9},{9,8},{10,11... | collective-permute-start | bytes 4718600 | tf_op jit(solution)/shard_map/ppermute | solution.py:679
  378.4 61.8 %collective-permute-start.20 = (bf16[16,1,32,1536]{3,2,0,1:T(8,128)(2,1)}, bf16[16,1,32,1536]{3,2,0,1:T(8,128)(2,1)}, u32[]{:S(2)}, u32[]{:S(2)}) collective-permute-start(bf16[16,1,32,1536]{3,2,0,1:T(8,128)(2,1)} %dynamic-slice_bitcast_fusion.4), channel_id=1, source_target_pairs={{0,1},{1,0},{2,3},{3,2},{4,5},{5,4},{6,7},{7,6},{8,9},{9,8},{10,11... | collective-permute-start | bytes 4718600 | tf_op jit(solution)/shard_map/ppermute | solution.py:679
  380.6 30.5 %collective-permute-start.38 = (bf16[2,1,32,2048]{3,2,0,1:T(8,128)(2,1)}, bf16[2,1,32,2048]{3,2,0,1:T(8,128)(2,1)}, u32[]{:S(2)}, u32[]{:S(2)}) collective-permute-start(bf16[2,1,32,2048]{3,2,0,1:T(8,128)(2,1)} %dynamic-slice_bitcast_fusion.20), channel_id=1, source_target_pairs={{0,8},{1,9},{2,10},{3,11},{4,12},{5,13},{6,14},{7,15},{8,0},{9,1},... | collective-permute-start | bytes 786440 | tf_op jit(solution)/shard_map/ppermute | solution.py:679
  383.1 31.0 %collective-permute-start.43 = (bf16[2,1,32,2048]{3,2,1,0:T(8,128)(2,1)S(1)}, bf16[2,1,32,2048]{3,2,1,0:T(8,128)(2,1)}, u32[]{:S(2)}, u32[]{:S(2)}) collective-permute-start(bf16[2,1,32,2048]{3,2,1,0:T(8,128)(2,1)S(1)} %dynamic-slice_bitcast_fusion.19), channel_id=1, source_target_pairs={{0,8},{1,9},{2,10},{3,11},{4,12},{5,13},{6,14},{7,15},{8,0},{9,1},... | collective-permute-start | bytes 786440 | tf_op jit(solution)/shard_map/ppermute | solution.py:679
  (86 other events, 1091.1 us)

commit v2 on v1

--- a/solution.py
+++ b/solution.py
@@ -360,6 +360,15 @@
 VMEM_LIMIT = 56 * 1024 * 1024
 NT = (((1,), (1,)), ((), ()))
 NN = (((1,), (0,)), ((), ()))
+
+
+def cost(microseconds):
+    return pl.CostEstimate(
+        flops=int(microseconds * 1e9), bytes_accessed=int(microseconds * 3e6), transcendentals=0
+    )
+
+
+ANYWHERE = pl.BlockSpec(memory_space=pl.ANY)
 
 
 def full_block(shape):
@@ -471,6 +480,7 @@
         compiler_params=pltpu.CompilerParams(
             vmem_limit_bytes=VMEM_LIMIT, dimension_semantics=("arbitrary",)
         ),
+        cost_estimate=cost(8),
         name="project_qkv",
     )(my_frames, tokens_here, mod_first, qkv_weight, qkv_weight, qkv_weight, *tables)
 
@@ -504,9 +514,22 @@
 
 
 def attend_kernel(
-    frames_ref, slots_ref, qkv_ref, att_ref, ot_ref, lse_ref, q_ref, k_ref, v_ref, vt_ref
+    frames_ref,
+    slots_ref,
+    qkv_ref,
+    first_ref,
+    after_ref,
+    att_ref,
+    ot_ref,
+    lse_ref,
+    copy_ref,
+    q_ref,
+    k_ref,
+    v_ref,
+    vt_ref,
 ):
     token_count = qkv_ref.shape[0]
+    copy_ref[...] = first_ref[...]
     by_frame(frames_ref, qkv_ref, (q_ref, k_ref, v_ref))
     vt_ref[:LANES, :] = v_ref[...].T
     vt_ref[LANES:, :] = jnp.ones((vt_ref.shape[0] - LANES, token_count), jnp.bfloat16)
@@ -538,11 +561,11 @@
         rounded = out.T.astype(jnp.bfloat16)
         for half in range(2):
             slot = slots_ref[2 * turn + half]
-            rows = pl.ds(pl.multiple_of(slot * PATCHES, PATCHES), PATCHES)
-            att_ref[rows, :] = rounded[half * PATCHES : (half + 1) * PATCHES, :]
-
-
-def attend(frames, slots, qkv):
+            rows = pl.ds(pl.multiple_of(slot % 2 * PATCHES, PATCHES), PATCHES)
+            att_ref[slot // 2, rows, :] = rounded[half * PATCHES : (half + 1) * PATCHES, :]
+
+
+def attend(frames, slots, qkv, first_in, after):
     token_count = qkv.shape[0]
     turns = token_count // (2 * PATCHES)
     return pl.pallas_call(
@@ -551,18 +574,22 @@
             pl.BlockSpec(memory_space=pltpu.SMEM),
             pl.BlockSpec(memory_space=pltpu.SMEM),
             pl.BlockSpec(memory_space=pltpu.VMEM),
+            pl.BlockSpec(memory_space=pltpu.VMEM),
+            ANYWHERE,
         ],
-        out_specs=[pl.BlockSpec(memory_space=pltpu.VMEM)] * 3,
+        out_specs=[pl.BlockSpec(memory_space=pltpu.VMEM)] * 4,
         out_shape=[
-            jax.ShapeDtypeStruct((token_count, LANES), jnp.bfloat16),
+            jax.ShapeDtypeStruct((turns, 2 * PATCHES, LANES), jnp.bfloat16),
             jax.ShapeDtypeStruct((LANES, token_count), jnp.float32),
             jax.ShapeDtypeStruct((turns, 4 * PATCHES), jnp.float32),
+            jax.ShapeDtypeStruct(first_in.shape, jnp.bfloat16),
         ],
         scratch_shapes=[pltpu.VMEM((token_count, LANES), jnp.bfloat16)] * 3
         + [pltpu.VMEM((LANES + 16, token_count), jnp.bfloat16)],
         compiler_params=pltpu.CompilerParams(vmem_limit_bytes=VMEM_LIMIT),
+        cost_estimate=cost(10),
         name="attend",
-    )(frames, slots, qkv)
+    )(frames, slots, qkv, first_in, after)
 
 
 def attend_back_kernel(
@@ -576,6 +603,7 @@
     fsin_ref,
     pcos_ref,
     psin_ref,
+    after_ref,
     out_ref,
     q_ref,
     k_ref,
@@ -592,8 +620,9 @@
     step = 2 * PATCHES
 
     def put(frame, part, values):
-        rows = pl.ds(pl.multiple_of(slots_ref[frame] * PATCHES, PATCHES), PATCHES)
-        out_ref[rows, part * LANES : (part + 1) * LANES] = values
+        slot = slots_ref[frame]
+        rows = pl.ds(pl.multiple_of(slot % 2 * PATCHES, PATCHES), PATCHES)
+        out_ref[slot // 2, rows, part * LANES : (part + 1) * LANES] = values
 
     def turn_back(frame, values):
         values = values.astype(jnp.bfloat16).astype(jnp.float32)
@@ -657,21 +686,24 @@
         put(frame, 2, dv_ref[rows, :].astype(jnp.bfloat16))
 
 
-def attend_back(frames, slots, qkv, grads, ot, lse, tables):
+def attend_back(frames, slots, qkv, grads, ot, lse, tables, after):
     token_count = qkv.shape[0]
     smem = pl.BlockSpec(memory_space=pltpu.SMEM)
     vmem = pl.BlockSpec(memory_space=pltpu.VMEM)
     return pl.pallas_call(
         attend_back_kernel,
-        in_specs=[smem, smem] + [vmem] * 8,
+        in_specs=[smem, smem] + [vmem] * 8 + [ANYWHERE],
         out_specs=vmem,
-        out_shape=jax.ShapeDtypeStruct((token_count, 3 * LANES), jnp.bfloat16),
+        out_shape=jax.ShapeDtypeStruct(
+            (token_count // (2 * PATCHES), 2 * PATCHES, 3 * LANES), jnp.bfloat16
+        ),
         scratch_shapes=[pltpu.VMEM((token_count, LANES), jnp.bfloat16)] * 4
         + [pltpu.VMEM((LANES, token_count), jnp.bfloat16)]
         + [pltpu.VMEM((token_count, LANES), jnp.float32)] * 2,
         compiler_params=pltpu.CompilerParams(vmem_limit_bytes=VMEM_LIMIT),
+        cost_estimate=cost(15),
         name="attend_back",
-    )(frames, slots, qkv, grads, ot, lse, *tables)
+    )(frames, slots, qkv, grads, ot, lse, *tables, after)
 
 
 def swap(values, bit):
@@ -680,42 +712,431 @@
 
 
 def gather_pairs(values):
-    bit = 1
-    while bit < lax.axis_size(AXES):
+    bit = lax.axis_size(AXES) // 2
+    while bit:
         values = jnp.concatenate([values, swap(values, bit)], axis=0)
-        bit *= 2
+        bit //= 2
     return values
 
 
-def halving_sum(values, order):
-    index = lax.axis_index(AXES)
-    left = sorted(order)
-    for position, bit in enumerate(order):
-        place = left.index(bit)
-        above = 2 ** (len(left) - 1 - place)
-        split = values.reshape((above, 2, 2**place) + values.shape[1:])
-        mine = (index >> bit) & 1
-        keep = lax.dynamic_index_in_dim(split, mine, 1, keepdims=False)
-        send = lax.dynamic_index_in_dim(split, 1 - mine, 1, keepdims=False)
-        got = swap(send, 2**bit)
-        total = keep.astype(jnp.float32) + got.astype(jnp.float32)
-        if position < len(order) - 1:
-            total = total.astype(jnp.bfloat16)
-        values = total.reshape((above * 2**place,) + values.shape[1:])
-        left.remove(bit)
-    return values[0]
-
-
-def sum_shares(values):
-    count = lax.axis_size(AXES)
-    rows, columns = values.shape
-    blocks = values.reshape(count, rows // count, columns)
-    bits = list(range(count.bit_length() - 1))
-    other = [0, 2, 1] + bits[3:]
-    half = columns // 2
-    return jnp.concatenate(
-        [halving_sum(blocks[:, :, :half], bits), halving_sum(blocks[:, :, half:], other)], axis=1
-    )
+HIDDEN_AT, UP_AT, SECOND_AT, MLP_AT, ATTENDED_AT, ATTN_AT, ACTS = (
+    0,
+    FF,
+    2 * FF,
+    2 * FF + D,
+    2 * FF + 2 * D,
+    2 * FF + 3 * D,
+    2 * FF + 4 * D,
+)
+FF_TILE = 512
+
+
+def middle_kernel(
+    att_ref,
+    tokens_ref,
+    cot_ref,
+    mod_ref,
+    ow_ref,
+    up_ref,
+    down_ref,
+    layer_ref,
+    acts_ref,
+    datt_ref,
+    dmid_ref,
+    dmod_ref,
+    attn_ref,
+    mid_ref,
+    mlp_ref,
+    dsec_ref,
+):
+    step = pl.program_id(0)
+    slot_rows = [slice(slot * PATCHES, (slot + 1) * PATCHES) for slot in range(2)]
+
+    def member(slot, which):
+        return mod_ref[slot : slot + 1, which * D : (which + 1) * D]
+
+    @pl.when(step == 0)
+    def _():
+        for group in range(D // LANES):
+            acts_ref[:, ATTENDED_AT + group * LANES : ATTENDED_AT + (group + 1) * LANES] = att_ref[
+                group
+            ]
+        attn_ref[...] = lax.dot_general(
+            acts_ref[:, ATTENDED_AT : ATTENDED_AT + D],
+            ow_ref[...],
+            NN,
+            preferred_element_type=jnp.float32,
+        )
+        for slot, rows in enumerate(slot_rows):
+            middle = tokens_ref[rows, :].astype(jnp.float32) + member(slot, 2) * attn_ref[rows, :]
+            mid_ref[rows, :] = middle
+            normed, unused = normalize(middle)
+            acts_ref[rows, SECOND_AT : SECOND_AT + D] = (
+                normed * (1.0 + member(slot, 4)) + member(slot, 3)
+            ).astype(jnp.bfloat16)
+            acts_ref[rows, MLP_AT : MLP_AT + D] = (
+                cot_ref[rows, :].astype(jnp.float32) * member(slot, 5)
+            ).astype(jnp.bfloat16)
+        mlp_ref[...] = jnp.zeros_like(mlp_ref)
+        dsec_ref[...] = jnp.zeros_like(dsec_ref)
+
+    up_lin = lax.dot_general(
+        acts_ref[:, SECOND_AT : SECOND_AT + D],
+        up_ref[...],
+        NN,
+        preferred_element_type=jnp.float32,
+    )
+    below = 0.5 + 0.5 * lax.erf(up_lin * 0.7071067811865476)
+    density = jnp.exp(up_lin * up_lin * -0.5) * 0.3989422804014327
+    hidden = (up_lin * below).astype(jnp.bfloat16)
+    d_hidden = lax.dot_general(
+        acts_ref[:, MLP_AT : MLP_AT + D], down_ref[...], NT, preferred_element_type=jnp.float32
+    )
+    d_up = (d_hidden * (below + up_lin * density)).astype(jnp.bfloat16)
+    acts_ref[:, pl.ds(pl.multiple_of(HIDDEN_AT + step * FF_TILE, FF_TILE), FF_TILE)] = hidden
+    acts_ref[:, pl.ds(pl.multiple_of(UP_AT + step * FF_TILE, FF_TILE), FF_TILE)] = d_up
+    mlp_ref[...] += lax.dot_general(
+        hidden, down_ref[...], NN, preferred_element_type=jnp.float32
+    )
+    dsec_ref[...] += lax.dot_general(d_up, up_ref[...], NT, preferred_element_type=jnp.float32)
+
+    @pl.when(step == pl.num_programs(0) - 1)
+    def _():
+        for slot, rows in enumerate(slot_rows):
+            middle = mid_ref[rows, :]
+            mlp_out = mlp_ref[rows, :]
+            cotangent = cot_ref[rows, :].astype(jnp.float32)
+            layer_ref[rows, :] = (middle + member(slot, 5) * mlp_out).astype(jnp.bfloat16)
+            normed, inverse = normalize(middle)
+            d_second = dsec_ref[rows, :]
+            d_middle = cotangent + norm_backward(
+                d_second * (1.0 + member(slot, 4)), normed, inverse
+            )
+            dmid_ref[rows, :] = d_middle
+            acts_ref[rows, ATTN_AT : ATTN_AT + D] = (d_middle * member(slot, 2)).astype(
+                jnp.bfloat16
+            )
+            for place, values in enumerate(
+                (d_middle * attn_ref[rows, :], d_second, d_second * normed, cotangent * mlp_out)
+            ):
+                dmod_ref[slot : slot + 1, place * D : (place + 1) * D] = jnp.sum(
+                    values, axis=0, keepdims=True
+                )
+        d_attended = lax.dot_general(
+            acts_ref[:, ATTN_AT : ATTN_AT + D],
+            ow_ref[...],
+            NT,
+            preferred_element_type=jnp.float32,
+        ).astype(jnp.bfloat16)
+        for group in range(D // LANES):
+            datt_ref[group] = d_attended[:, group * LANES : (group + 1) * LANES]
+
+
+def middle_block(att, tokens_here, cot_here, modulation, out_weight, fc1_weight, fc2_weight):
+    rows = tokens_here.shape[0]
+    return pl.pallas_call(
+        middle_kernel,
+        grid=(FF // FF_TILE,),
+        in_specs=[
+            full_block(att.shape),
+            full_block((rows, D)),
+            full_block((rows, D)),
+            full_block(modulation.shape),
+            full_block((D, D)),
+            pl.BlockSpec((D, FF_TILE), lambda f: (0, f)),
+            pl.BlockSpec((FF_TILE, D), lambda f: (f, 0)),
+        ],
+        out_specs=[
+            full_block((rows, D)),
+            full_block((rows, ACTS)),
+            full_block(att.shape),
+            full_block((rows, D)),
+            full_block((2, 4 * D)),
+        ],
+        out_shape=[
+            jax.ShapeDtypeStruct((rows, D), jnp.bfloat16),
+            jax.ShapeDtypeStruct((rows, ACTS), jnp.bfloat16),
+            jax.ShapeDtypeStruct(att.shape, jnp.bfloat16),
+            jax.ShapeDtypeStruct((rows, D), jnp.float32),
+            jax.ShapeDtypeStruct((2, 4 * D), jnp.float32),
+        ],
+        scratch_shapes=[pltpu.VMEM((rows, D), jnp.float32)] * 4,
+        compiler_params=pltpu.CompilerParams(
+            vmem_limit_bytes=VMEM_LIMIT, dimension_semantics=("arbitrary",)
+        ),
+        cost_estimate=cost(21),
+        name="middle_block",
+    )(att, tokens_here, cot_here, modulation, out_weight, fc1_weight, fc2_weight)
+
+
+CHIPS = 16
+TILE = 256
+SHARE_ROWS = (FF + 4 * D + D) // TILE * D // CHIPS // 4
+
+
+def weight_kernel(
+    bits_ref, mine_ref, theirs_ref, keep_a, send_a, keep_b, send_b, left1_ref, left2_ref, left3_ref
+):
+    core, xbit, ybit = bits_ref[0], bits_ref[1], bits_ref[2]
+    rows = mine_ref.shape[0]
+    small = D // CHIPS // 2
+    for place, ref in enumerate((mine_ref, theirs_ref)):
+        columns = slice(place * rows, (place + 1) * rows)
+        for source, target in ((SECOND_AT, left1_ref), (ATTENDED_AT, left3_ref)):
+            turned = ref[:, source : source + D].T.reshape(CHIPS, 2, small, rows)
+            target[:, columns] = jnp.where(core == 0, turned[:, 0], turned[:, 1]).reshape(
+                D // 2, rows
+            )
+        for chip in range(CHIPS):
+            source = pl.multiple_of(HIDDEN_AT + (2 * chip + core) * LANES, LANES)
+            left2_ref[chip * LANES : (chip + 1) * LANES, columns] = ref[:, pl.ds(source, LANES)].T
+
+    jobs = []
+    at = [0, 0]
+    for left, right_at, width, height in (
+        (left1_ref, UP_AT, FF, small),
+        (left2_ref, MLP_AT, D, LANES),
+        (left3_ref, ATTN_AT, D, small),
+    ):
+        tiles = width // TILE
+        for tile in range(tiles):
+            second = tile >= tiles // 2
+            jobs.append((left, right_at + tile * TILE, height, second, at[second]))
+            at[second] += height
+    for left, source, height, second, place in jobs:
+        right = jnp.concatenate(
+            [mine_ref[:, source : source + TILE], theirs_ref[:, source : source + TILE]], axis=0
+        )
+        part = lax.dot_general(
+            left[...], right, NN, preferred_element_type=jnp.float32
+        ).astype(jnp.bfloat16)
+        out_rows = slice(place, place + height)
+        if second:
+            part = part.reshape(CHIPS // 4, 2, 2, height, TILE)
+            low, high, chosen = part[:, 0], part[:, 1], ybit
+            keep_b[:, :, out_rows, :] = jnp.where(chosen == 0, low, high)
+            send_b[:, :, out_rows, :] = jnp.where(chosen == 0, high, low)
+        else:
+            part = part.reshape(CHIPS // 2, 2, height, TILE)
+            low, high, chosen = part[:, 0], part[:, 1], xbit
+            keep_a[:, out_rows, :] = jnp.where(chosen == 0, low, high)
+            send_a[:, out_rows, :] = jnp.where(chosen == 0, high, low)
+
+
+def weight_parts(bits, mine, theirs):
+    rows = mine.shape[0]
+    vmem = pl.BlockSpec(memory_space=pltpu.VMEM)
+    first = jax.ShapeDtypeStruct((CHIPS // 2, SHARE_ROWS, TILE), jnp.bfloat16)
+    second = jax.ShapeDtypeStruct((CHIPS // 4, 2, SHARE_ROWS, TILE), jnp.bfloat16)
+    return pl.pallas_call(
+        weight_kernel,
+        in_specs=[pl.BlockSpec(memory_space=pltpu.SMEM), vmem, vmem],
+        out_specs=[vmem] * 4,
+        out_shape=[first, first, second, second],
+        scratch_shapes=[
+            pltpu.VMEM((D // 2, 2 * rows), jnp.bfloat16),
+            pltpu.VMEM((FF // 2, 2 * rows), jnp.bfloat16),
+            pltpu.VMEM((D // 2, 2 * rows), jnp.bfloat16),
+        ],
+        compiler_params=pltpu.CompilerParams(vmem_limit_bytes=VMEM_LIMIT),
+        cost_estimate=cost(13),
+        name="weight_parts",
+    )(bits, mine, theirs)
+
+
+def first_back_kernel(
+    dqkv_ref,
+    tokens_ref,
+    mod_ref,
+    dmid_ref,
+    qw_ref,
+    kw_ref,
+    vw_ref,
+    after_ref,
+    grad_ref,
+    late_ref,
+    total_ref,
+):
+    step = pl.program_id(0)
+    weights = jnp.concatenate([qw_ref[...], kw_ref[...], vw_ref[...]], axis=1)
+    update = lax.dot_general(dqkv_ref[0], weights, NT, preferred_element_type=jnp.float32)
+
+    @pl.when(step == 0)
+    def _():
+        total_ref[...] = update
+
+    @pl.when(step > 0)
+    def _():
+        total_ref[...] += update
+
+    @pl.when(step == pl.num_programs(0) - 1)
+    def _():
+        for slot in range(2):
+            rows = slice(slot * PATCHES, (slot + 1) * PATCHES)
+            normed, inverse = normalize(tokens_ref[rows, :].astype(jnp.float32))
+            d_first = total_ref[rows, :]
+            scale = mod_ref[slot : slot + 1, D : 2 * D]
+            grad_ref[rows, :] = (
+                dmid_ref[rows, :] + norm_backward(d_first * (1.0 + scale), normed, inverse)
+            ).astype(jnp.bfloat16)
+            late_ref[slot : slot + 1, :D] = jnp.sum(d_first, axis=0, keepdims=True)
+            late_ref[slot : slot + 1, D:] = jnp.sum(d_first * normed, axis=0, keepdims=True)
+
+
+def first_back(d_qkv, tokens_here, modulation, d_middle, qkv_weight, after):
+    groups, rows, width = d_qkv.shape
+    weight_specs = [
+        pl.BlockSpec((D, LANES), lambda g, part=part: (0, part * groups + g)) for part in range(3)
+    ]
+    return pl.pallas_call(
+        first_back_kernel,
+        grid=(groups,),
+        in_specs=[
+            pl.BlockSpec((1, rows, width), lambda g: (g, 0, 0)),
+            full_block((rows, D)),
+            full_block(modulation.shape),
+            full_block((rows, D)),
+        ]
+        + weight_specs
+        + [ANYWHERE],
+        out_specs=[full_block((rows, D)), full_block((2, 2 * D))],
+        out_shape=[
+            jax.ShapeDtypeStruct((rows, D), jnp.bfloat16),
+            jax.ShapeDtypeStruct((2, 2 * D), jnp.float32),
+        ],
+        scratch_shapes=[pltpu.VMEM((rows, D), jnp.float32)],
+        compiler_params=pltpu.CompilerParams(
+            vmem_limit_bytes=VMEM_LIMIT, dimension_semantics=("arbitrary",)
+        ),
+        cost_estimate=cost(9),
+        name="first_back",
+    )(d_qkv, tokens_here, modulation, d_middle, qkv_weight, qkv_weight, qkv_weight, after)
+
+
+def add_split(keep, got, axis, bit):
+    def pick(which):
+        return (
+            lax.dynamic_index_in_dim(keep, which, axis, keepdims=False).astype(jnp.float32)
+            + lax.dynamic_index_in_dim(got, which, axis, keepdims=False).astype(jnp.float32)
+        ).astype(jnp.bfloat16)
+
+    return pick(bit), pick(1 - bit)
+
+
+def qkv_part_kernel(core_ref, first_ref, grad_ref, after_ref, keep_ref, send_ref, total_ref):
+    step = pl.program_id(0)
+    update = lax.dot_general(
+        first_ref[...], grad_ref[...], (((0,), (0,)), ((), ())), preferred_element_type=jnp.float32
+    )
+
+    @pl.when(step == 0)
+    def _():
+        total_ref[...] = update
+
+    @pl.when(step > 0)
+    def _():
+        total_ref[...] += update
+
+    @pl.when(step == pl.num_programs(0) - 1)
+    def _():
+        groups, clip_pairs, share, width = keep_ref.shape
+        split = total_ref[...].astype(jnp.bfloat16).reshape(groups, clip_pairs, 2, share, width)
+        low, high = split[:, :, 0], split[:, :, 1]
+        keep_ref[...] = jnp.where(core_ref[0] == 0, low, high)
+        send_ref[...] = jnp.where(core_ref[0] == 0, high, low)
+
+
+def qkv_parts(core, first_all, d_heads, share, after):
+    rows, width = d_heads.shape
+    tile = 512
+    shape = (D // LANES, 2, share, width)
+    return pl.pallas_call(
+        qkv_part_kernel,
+        grid_spec=pltpu.PrefetchScalarGridSpec(
+            num_scalar_prefetch=1,
+            grid=(rows // tile,),
+            in_specs=[
+                pl.BlockSpec((tile, D), lambda i, core: (i, 0)),
+                pl.BlockSpec((tile, width), lambda i, core: (i, 0)),
+                ANYWHERE,
+            ],
+            out_specs=[full_block(shape)] * 2,
+            scratch_shapes=[pltpu.VMEM((D, width), jnp.float32)],
+        ),
+        out_shape=[jax.ShapeDtypeStruct(shape, jnp.bfloat16)] * 2,
+        compiler_params=pltpu.CompilerParams(
+            vmem_limit_bytes=VMEM_LIMIT, dimension_semantics=("arbitrary",)
+        ),
+        cost_estimate=cost(5),
+        name="qkv_parts",
+    )(core, first_all, d_heads, after)
+
+
+def fold_kernel(bits_ref, keep_a, got_a, keep_b, got_b, after_ref, *out_refs):
+    for place, (keep, got) in enumerate(((keep_a, got_a), (keep_b, got_b))):
+        low, high = (
+            (
+                keep[0, half].astype(jnp.float32) + got[0, half].astype(jnp.float32)
+            ).astype(jnp.bfloat16)
+            for half in range(2)
+        )
+        kept, sent = out_refs[2 * place : 2 * place + 2]
+        kept[0] = jnp.where(bits_ref[place] == 0, low, high)
+        sent[0] = jnp.where(bits_ref[place] == 0, high, low)
+
+
+def fold(bits, keep_a, got_a, keep_b, got_b, after):
+    count, unused, rows, columns = keep_a.shape
+    parts = 1 if count > 1 else 3
+    in_block = pl.BlockSpec((1, 2, rows // parts, columns), lambda i, j, bits: (i, 0, j, 0))
+    out_block = pl.BlockSpec((1, rows // parts, columns), lambda i, j, bits: (i, j, 0))
+    out = jax.ShapeDtypeStruct((count, rows, columns), jnp.bfloat16)
+    return pl.pallas_call(
+        fold_kernel,
+        grid_spec=pltpu.PrefetchScalarGridSpec(
+            num_scalar_prefetch=1,
+            grid=(count, parts),
+            in_specs=[in_block] * 4 + [ANYWHERE],
+            out_specs=[out_block] * 4,
+        ),
+        out_shape=[out] * 4,
+        compiler_params=pltpu.CompilerParams(
+            vmem_limit_bytes=VMEM_LIMIT, dimension_semantics=("arbitrary", "arbitrary")
+        ),
+        cost_estimate=cost(1 + count),
+        name="fold",
+    )(jnp.stack(bits), keep_a, got_a, keep_b, got_b, after)
+
+
+def finish_kernel(keep_a, got_a, keep_b, got_b, upper_ref, lower_ref, outw_ref):
+    for place, (keep, got) in enumerate(((keep_a, got_a), (keep_b, got_b))):
+        row = 0
+        for target in (upper_ref, lower_ref, outw_ref):
+            height, width = target.shape
+            tiles = width // 2 // TILE
+            for tile in range(tiles):
+                column = (place * tiles + tile) * TILE
+                target[:, column : column + TILE] = keep[row : row + height, :].astype(
+                    jnp.float32
+                ) + got[row : row + height, :].astype(jnp.float32)
+                row += height
+
+
+def finish(share, keep_a, got_a, keep_b, got_b):
+    vmem = pl.BlockSpec(memory_space=pltpu.VMEM)
+    return pl.pallas_call(
+        finish_kernel,
+        in_specs=[vmem] * 4,
+        out_specs=[vmem] * 3,
+        out_shape=[
+            jax.ShapeDtypeStruct((share, FF), jnp.float32),
+            jax.ShapeDtypeStruct((FF * share // D, D), jnp.float32),
+            jax.ShapeDtypeStruct((share, D), jnp.float32),
+        ],
+        compiler_params=pltpu.CompilerParams(vmem_limit_bytes=VMEM_LIMIT),
+        cost_estimate=cost(2),
+        name="finish",
+    )(keep_a, got_a, keep_b, got_b)
 
 
 def local_heads(
@@ -734,12 +1155,23 @@
     rows_here = 2 * PATCHES
     frame_count = group_map.shape[0]
     groups = D // LANES
-    clips = lax.axis_size("clip")
     device_count = lax.axis_size(AXES)
     index = lax.axis_index(AXES)
+    bits = [(index >> place) & 1 for place in range(5)]
     slots = jnp.argsort(group_map).astype(jnp.int32)
     my_frames = lax.dynamic_slice_in_dim(group_map, 2 * lax.axis_index("blk"), 2)
     tables = rope_tables(frame_count)
+    clip_levels = noise_levels
+    for bit in (1, 2):
+        clip_levels = jnp.concatenate([clip_levels, swap(clip_levels, bit)], axis=0)
+    members = jnp.zeros((1,), jnp.int32)
+    for bit in (16, 8, 4, 2, 1):
+        members = jnp.concatenate([members, members ^ bit])
+    member_slots = (2 * ((index ^ members) >> 2))[:, None] + jnp.arange(2, dtype=jnp.int32)[None, :]
+    levels_all = clip_levels[(members & 3)[:, None], group_map[member_slots]].reshape(
+        2 * device_count
+    )
+    tokens_here = tokens.reshape(rows_here, D)
     embedded = jnp.concatenate(
         [
             lax.dynamic_slice_in_dim(noise_table, noise_levels[0, my_frames[slot]], 1)
@@ -751,92 +1183,68 @@
         jnp.dot(activated, mod_weight, preferred_element_type=jnp.float32)
         + mod_bias.astype(jnp.float32)[None, :]
     )
-    shift_one, scale_one, gate_one, shift_two, scale_two, gate_two = [
-        modulation[:, member * D : (member + 1) * D][:, None, :] for member in range(6)
-    ]
     qkv_out, first_in = project_qkv(
-        my_frames, tokens.reshape(rows_here, D), modulation[:, : 2 * D], qkv_weight, tables
+        my_frames, tokens_here, modulation[:, : 2 * D], qkv_weight, tables
     )
     qkv_heads = lax.all_to_all(qkv_out, "blk", 0, 0, tiled=True).reshape(-1, 3 * LANES)
-    att_heads, ot, lse = attend(group_map, slots, qkv_heads)
-    attended_low = (
-        lax.all_to_all(att_heads.reshape(groups, rows_here, LANES), "blk", 0, 0, tiled=True)
-        .transpose(1, 0, 2)
-        .reshape(rows_here, D)
-    )
-    inputs_here = tokens[0].astype(jnp.float32)
-    attn_out = jnp.dot(attended_low, out_weight, preferred_element_type=jnp.float32).reshape(
-        2, PATCHES, D
-    )
-    middle = inputs_here + gate_one * attn_out
-    normed_two, inverse_two = normalize(middle)
-    second_in = (
-        (normed_two * (1.0 + scale_two) + shift_two).astype(jnp.bfloat16).reshape(rows_here, D)
-    )
-    up_lin = jnp.dot(second_in, fc1_weight, preferred_element_type=jnp.float32)
-    hidden = jax.nn.gelu(up_lin, approximate=False).astype(jnp.bfloat16)
-    mlp_out = jnp.dot(hidden, fc2_weight, preferred_element_type=jnp.float32).reshape(2, PATCHES, D)
-    layer_out = (middle + gate_two * mlp_out).astype(jnp.bfloat16)[None]
-    cotangent = out_cotangent[0].astype(jnp.float32)
-    d_gate_two = jnp.sum(cotangent * mlp_out, axis=1)
-    d_mlp = (cotangent * gate_two).astype(jnp.bfloat16).reshape(rows_here, D)
-    lower_part = jnp.einsum("rf,rd->fd", hidden, d_mlp, preferred_element_type=jnp.float32)
-    lower_share = sum_shares(lower_part.astype(jnp.bfloat16))
-    d_hidden = jnp.einsum("rd,fd->rf", d_mlp, fc2_weight, preferred_element_type=jnp.float32)
-    unused_value, gelu_pull = jax.vjp(partial(jax.nn.gelu, approximate=False), up_lin)
-    d_up = gelu_pull(d_hidden)[0].astype(jnp.bfloat16)
-    upper_part = jnp.einsum("rc,rf->cf", second_in, d_up, preferred_element_type=jnp.float32)
-    upper_share = sum_shares(upper_part.astype(jnp.bfloat16))
-    d_second = jnp.einsum(
-        "rf,cf->rc", d_up, fc1_weight, preferred_element_type=jnp.float32
-    ).reshape(2, PATCHES, D)
-    d_shift_two = jnp.sum(d_second, axis=1)
-    d_scale_two = jnp.sum(d_second * normed_two, axis=1)
-    d_middle = cotangent + norm_backward(d_second * (1.0 + scale_two), normed_two, inverse_two)
-    d_gate_one = jnp.sum(d_middle * attn_out, axis=1)
-    d_attn = (d_middle * gate_one).astype(jnp.bfloat16).reshape(rows_here, D)
-    outw_part = jnp.einsum("rc,rd->cd", attended_low, d_attn, preferred_element_type=jnp.float32)
-    outw_share = sum_shares(outw_part.astype(jnp.bfloat16))
-    d_attended = jnp.einsum(
-        "rd,cd->rc", d_attn, out_weight, preferred_element_type=jnp.float32
-    ).astype(jnp.bfloat16)
-    early_all = gather_pairs(
-        jnp.concatenate([d_gate_one, d_shift_two, d_scale_two, d_gate_two], axis=1).astype(
-            jnp.bfloat16
-        )[None]
-    )
-    grad_heads = lax.all_to_all(
-        d_attended.reshape(rows_here, groups, LANES).transpose(1, 0, 2), "blk", 0, 0, tiled=True
-    ).reshape(-1, LANES)
-    d_heads = attend_back(group_map, slots, qkv_heads, grad_heads, ot, lse, tables)
-    d_qkv = (
-        lax.all_to_all(d_heads.reshape(groups, rows_here, 3 * LANES), "blk", 0, 0, tiled=True)
-        .reshape(groups, rows_here, 3, LANES)
+    att_heads, ot, lse, first_in = attend(group_map, slots, qkv_heads, first_in, levels_all)
+    att = lax.all_to_all(att_heads, "blk", 0, 0, tiled=True)
+    first_all = lax.all_gather(first_in, "blk", axis=0, tiled=True)
+    layer_out, acts, d_att, d_middle, d_mod_early = middle_block(
+        att,
+        tokens_here,
+        out_cotangent.reshape(rows_here, D),
+        modulation,
+        out_weight,
+        fc1_weight,
+        fc2_weight,
+    )
+    grad_heads = lax.all_to_all(d_att, "blk", 0, 0, tiled=True).reshape(-1, LANES)
+    acts_other = swap(acts, 1)
+    keep_a, send_a, keep_b, send_b = weight_parts(jnp.stack(bits[:3]), acts, acts_other)
+    got_a, got_b = swap(send_a, 2), swap(send_b, 4)
+    d_heads = attend_back(group_map, slots, qkv_heads, grad_heads, ot, lse, tables, send_a)
+    d_qkv = lax.all_to_all(d_heads, "blk", 0, 0, tiled=True)
+    share = D // device_count
+    split = (-1, 2, SHARE_ROWS, TILE)
+    keep_a, send_a, keep_b, send_b = fold(
+        [bits[2], bits[1]],
+        keep_a.reshape(split),
+        got_a.reshape(split),
+        keep_b,
+        got_b,
+        d_heads,
+    )
+    got_a, got_b = swap(send_a, 4), swap(send_b, 2)
+    tokens_grad, d_mod_late = first_back(
+        d_qkv, tokens_here, modulation, d_middle, qkv_weight, send_a
+    )
+    qkv_keep, qkv_send = qkv_parts(
+        bits[0].reshape(1), first_all, d_heads.reshape(-1, 3 * LANES), share, d_mod_late
+    )
+    qkv_keep, qkv_send = add_split(qkv_keep, swap(qkv_send, 1), 1, bits[1])
+    qkv_got = swap(qkv_send, 2)
+    qkv_sum = (qkv_keep.astype(jnp.float32) + qkv_got.astype(jnp.float32)).astype(jnp.bfloat16)
+    qkv_share = (
+        lax.all_to_all(qkv_sum, "blk", 0, 0, tiled=True)
+        .reshape(groups, share, 3, LANES)
         .transpose(1, 2, 0, 3)
-        .reshape(rows_here, 3 * D)
-    )
-    qkv_part = jnp.einsum("rc,rk->ck", first_in, d_qkv, preferred_element_type=jnp.float32)
-    qkv_share = sum_shares(qkv_part.astype(jnp.bfloat16))
-    d_first = jnp.einsum(
-        "rk,ck->rc", d_qkv, qkv_weight, preferred_element_type=jnp.float32
-    ).reshape(2, PATCHES, D)
-    normed_one, inverse_one = normalize(inputs_here)
-    d_shift_one = jnp.sum(d_first, axis=1)
-    d_scale_one = jnp.sum(d_first * normed_one, axis=1)
-    tokens_grad = (
-        d_middle + norm_backward(d_first * (1.0 + scale_one), normed_one, inverse_one)
-    ).astype(jnp.bfloat16)[None]
-    late_all = gather_pairs(
-        jnp.concatenate([d_shift_one, d_scale_one], axis=1).astype(jnp.bfloat16)[None]
-    )
-    d_mod_all = jnp.concatenate([late_all, early_all], axis=2).reshape(2 * device_count, 6 * D)
-    member_index = index ^ jnp.arange(device_count, dtype=jnp.int32)
-    levels_all = gather_pairs(
-        lax.dynamic_slice_in_dim(
-            jnp.broadcast_to(noise_levels[0][my_frames][:, None], (2, LANES)), 0, 2
-        )[None]
-    )[:, :, 0].reshape(2 * device_count)
-    share = D // device_count
+        .reshape(share, 3 * D)
+        .astype(jnp.float32)
+    )
+    for bit in (8, 16):
+        place = bit.bit_length() - 1
+        keep_a, send_a, keep_b, send_b = fold(
+            [bits[place], bits[place]],
+            *(part.reshape(split) for part in (keep_a, got_a, keep_b, got_b)),
+            d_mod_late,
+        )
+        got_a, got_b = swap(send_a, bit), swap(send_b, bit)
+    upper_share, lower_share, outw_share = finish(
+        share, *(part.reshape(SHARE_ROWS, TILE) for part in (keep_a, got_a, keep_b, got_b))
+    )
+    d_mod = jnp.concatenate([d_mod_late, d_mod_early], axis=1).astype(jnp.bfloat16)
+    d_mod_all = gather_pairs(d_mod[None]).reshape(2 * device_count, 6 * D)
     level_hot = jnp.arange(LEVELS, dtype=jnp.int32)[:, None] == levels_all[None, :]
     table_columns = lax.dynamic_slice_in_dim(noise_table, index * share, share, 1)
     embedded_columns = jnp.einsum(
@@ -866,8 +1274,8 @@
         axis=0,
     )
     return (
-        layer_out,
-        tokens_grad,
+        layer_out[None].reshape(1, 2, PATCHES, D),
+        tokens_grad.reshape(1, 2, PATCHES, D),
         table_share,
         modw_share,
         bias_share,
@@ -879,7 +1287,7 @@
 
 
 def solution(mesh):
-    pair_split = mesh.shape["blk"] * LANES == D
+    pair_split = mesh.shape["blk"] * LANES == D and mesh.shape["clip"] == 4
     return jax.shard_map(
         local_heads if pair_split else local,
         mesh=mesh,

time: 496 us -> 379 us (0.76)
  Pallas kernels: 35.6 us -> 104 us
  waiting for transfers between devices: 208 us -> 155 us
  matrix products: 62.9 us -> 11.2 us
  local copies, waits for them, and re-layouts: 53.3 us -> 14.7 us
  starting transfers between devices: 73.9 us -> 37.8 us
  other arithmetic: 42.3 us -> 9.87 us
  blocking collectives: 0 us -> 18.6 us
  between operations: 10.3 us -> 22.3 us
    pallas_call x1 -> x9, Pallas kernels: 15.3 us -> 83.5 us  [the longest x1 20.6 us: middle_block(): pl.pallas_call(middle_kernel, grid=(FF // FF_TILE,), in_specs=[full_block...]
    ppermute x55 -> x18, waiting for transfers between devices: 179 us -> 123 us  [swap(): lax.ppermute(values, AXES, [(index, index ^ bit) for index in range(count)])]
    dot_general x11 -> x0, matrix products: 51 us -> none  [the longest x1 13.3 us: local_heads(): jnp.einsum('rd,fd->rf', d_mlp, fc2_weight, preferred_element_type=jnp.flo...]
    ppermute x55 -> x18, starting transfers between devices: 53.3 us -> 17.4 us  [swap(): lax.ppermute(values, AXES, [(index, index ^ bit) for index in range(count)])]
    convert_element_type x36 -> x2, other arithmetic: 29 us -> 1.75 us  [the longest x1 0.99 us: pick(): return (lax.dynamic_index_in_dim(keep, which, axis, keepdims=False).astyp...]
    all_to_all x0 -> x1, blocking collectives: none -> 18.6 us  [local_heads(): att = lax.all_to_all(att_heads, 'blk', 0, 0, tiled=True)]
    squeeze x40 -> x0, local copies, waits for them, and re-layouts: 15.7 us -> none  [halving_sum(): send = lax.dynamic_index_in_dim(split, 1 - mine, 1, keepdims=False)]
    slice x5 -> x0, local copies, waits for them, and re-layouts: 15.5 us -> none  [the longest x4 15.2 us: sum_shares(): blocks[:, :, :half]]
  transfers between devices with their start and end apart: 59 -> 23, of which waited for: 36 -> 14; matrix products, arithmetic and copies ran while one was open for 19% -> 5% of each run, Pallas kernels for 5% -> 16%
where the time goes in v2:
time: 379 us; the launch traced here: 374 us
  waiting for transfers between devices  155 us (41%)
  Pallas kernels  104 us (27%)
  starting transfers between devices  37.8 us (10%)
  between operations  22.3 us (6%)
  blocking collectives  18.6 us (5%)
  local copies, waits for them, and re-layouts  14.7 us (4%)
  matrix products  11.2 us (3%)
  other arithmetic  9.87 us (3%)
    ppermute x18, waiting for transfers between devices, swap(): lax.ppermute(values, AXES, [(index, index ^ bit) for index in range(count)])  123 us
    all_to_all x1, waiting for transfers between devices, local_heads(): lax.all_to_all(qkv_out, 'blk', 0, 0, tiled=True).reshape(-1, 3 * LANES)  30.3 us
    pallas_call x1, Pallas kernels, middle_block(): pl.pallas_call(middle_kernel, grid=(FF // FF_TILE,), in_specs=[full_block...  20.6 us
    all_to_all x1, blocking collectives, local_heads(): att = lax.all_to_all(att_heads, 'blk', 0, 0, tiled=True)  18.6 us
    ppermute x18, starting transfers between devices, swap(): lax.ppermute(values, AXES, [(index, index ^ bit) for index in range(count)])  17.4 us
    pallas_call x1, Pallas kernels, attend_back(): pl.pallas_call(attend_back_kernel, in_specs=[smem, smem] + [vmem] * 8 + [...  15.5 us
    pallas_call x3, Pallas kernels, fold(): pl.pallas_call(fold_kernel, grid_spec=pltpu.PrefetchScalarGridSpec(num_sc...  15.3 us
    pallas_call x1, Pallas kernels, weight_parts(): pl.pallas_call(weight_kernel, in_specs=[pl.BlockSpec(memory_space=pltpu.S...  13.3 us
  transfers between devices with their start and end apart: 23, of which 14 were waited for; matrix products, arithmetic and copies ran while one was open for 5% of the time, Pallas kernels for 16%

profile of v2, /device:TPU:0, one launch (start us, length us, event | category | flops | bytes accessed | tf_op | source)
XLA Modules:
  0.0 373.9 jit_solution(5915896938467982455)
XLA Ops:
  19.1 6.3 %convolution_add_fusion.mod_ref = f32[2,6144]{1,0:T(2,128)S(1)} fusion(bf16[1024,6144]{1,0:T(8,128)(2,1)} %param.15, f32[6144]{0:T(1024)S(1)} %convert_element_type.80, bf16[1,1024]{1,0:T(2,128)(2,1)S(1)} %get-tuple-element.80, bf16[1,1024]{1,0:T(2,128)(2,1)S(1)} %get-tuple-element.79), kind=kOutput, calls=%fused_computation.2 | convolution fusion | flops 25196544 | bytes 12660736 | tf_op jit(solution)/shard_map/dot_general | solution.py:1183
  27.9 9.9 %project_qkv.1 = (bf16[8,256,384]{2,1,0:T(8,128)(2,1)}, bf16[256,1024]{1,0:T(8,128)(2,1)}) custom-call(s32[2]{0:T(128)} %copy-done.9, bf16[256,1024]{1,0:T(8,128)(2,1)} %bitcast.67, f32[2,2048]{1,0:T(2,128)} %slice.16.mod_ref, bf16[1024,3072]{1,0:T(8,128)(2,1)} %vw_ref.3, bf16[1024,3072]{1,0:T(8,128)(2,1)} %vw_ref.3, bf16[1024,3072]{1,0:T(8,128)(2,1)} %vw_ref.3, ...), custom_call_target="tpu_custom_call" | custom-call | flops 8000000000 | bytes 24000000 | tf_op jit(solution)/shard_map/project_qkv/pallas_call | solution.py:463
  37.8 7.4 %all-to-all-start = ((bf16[8,256,384]{2,1,0:T(8,128)(2,1)}), bf16[8,256,384]{2,1,0:T(8,128)(2,1)S(1)}, u32[]{:S(2)}, u32[]{:S(2)}) async-start(bf16[8,256,384]{2,1,0:T(8,128)(2,1)} %get-tuple-element.45), calls=%async_computation | async-start | bytes 3145728 | tf_op jit(solution)/shard_map/all_to_all | solution.py:1189
  51.9 30.3 %all-to-all-done = bf16[8,256,384]{2,1,0:T(8,128)(2,1)S(1)} async-done(((bf16[8,256,384]{2,1,0:T(8,128)(2,1)}), bf16[8,256,384]{2,1,0:T(8,128)(2,1)S(1)}, u32[]{:S(2)}, u32[]{:S(2)}) %all-to-all-start) | async-done | bytes 1572896 | tf_op jit(solution)/shard_map/all_to_all | solution.py:1189
  83.4 10.6 %attend.1 = (bf16[8,256,128]{2,1,0:T(8,128)(2,1)}, f32[128,2048]{1,0:T(8,128)}, f32[8,512]{1,0:T(8,128)}, bf16[256,1024]{1,0:T(8,128)(2,1)}) custom-call(s32[16]{0:T(128)} %frames_ref.3, s32[16]{0:T(128)} %get-tuple-element.44.slots_ref, bf16[2048,384]{1,0:T(8,128)(2,1)} %bitcast.57, bf16[256,1024]{1,0:T(8,128)(2,1)} %get-tuple-element.46.first_ref, ...), custom_call_target="tpu_custom_call" | custom-call | flops 10000000000 | bytes 30000000 | tf_op jit(solution)/shard_map/attend/pallas_call | solution.py:571
  94.0 18.6 %all_to_all.25.att_ref = bf16[8,256,128]{2,1,0:T(8,128)(2,1)} all-to-all(bf16[8,256,128]{2,1,0:T(8,128)(2,1)} %get-tuple-element.47), channel_id=1, replica_groups=mesh['blk'=8,'clip'=4] {'blk'}, dimensions={0} | all-to-all | bytes 1048576 | tf_op jit(solution)/shard_map/all_to_all | solution.py:1191
  112.6 20.6 %middle_block.1 = (bf16[256,1024]{1,0:T(8,128)(2,1)}, bf16[256,12288]{1,0:T(8,128)(2,1)}, bf16[8,256,128]{2,1,0:T(8,128)(2,1)}, f32[256,1024]{1,0:T(8,128)}, f32[2,4096]{1,0:T(2,128)}) custom-call(bf16[8,256,128]{2,1,0:T(8,128)(2,1)} %all_to_all.25.att_ref, bf16[256,1024]{1,0:T(8,128)(2,1)} %bitcast.68, bf16[256,1024]{1,0:T(8,128)(2,1)} %bitcast.66, ...), custom_call_target="tpu_custom_call" | custom-call | flops 20999999488 | bytes 63000000 | tf_op jit(solution)/shard_map/middle_block/pallas_call | solution.py:837
  137.6 6.1 %collective-permute-done.2.theirs_ref = bf16[256,12288]{1,0:T(8,128)(2,1)} collective-permute-done((bf16[256,12288]{1,0:T(8,128)(2,1)}, bf16[256,12288]{1,0:T(8,128)(2,1)}, u32[]{:S(2)}, u32[]{:S(2)}) %collective-permute-start.2) | collective-permute-done | bytes 6291488 | tf_op jit(solution)/shard_map/ppermute | solution.py:711
  143.7 13.3 %weight_parts.1 = (bf16[8,576,256]{2,1,0:T(8,128)(2,1)}, bf16[8,576,256]{2,1,0:T(8,128)(2,1)}, bf16[4,2,576,256]{3,2,1,0:T(8,128)(2,1)}, bf16[4,2,576,256]{3,2,1,0:T(8,128)(2,1)}) custom-call(s32[3]{0:T(128)} %pad_add_fusion.2.bits_ref, bf16[256,12288]{1,0:T(8,128)(2,1)} %get-tuple-element.52.mine_ref, bf16[256,12288]{1,0:T(8,128)(2,1)} %collective-permute-done.2.theirs_ref), custom_call_target="tpu_custom_call" | custom-call | flops 12999999488 | bytes 39000000 | tf_op jit(solution)/shard_map/weight_parts/pallas_call | solution.py:931
  162.6 15.5 %attend_back.1.after_ref = bf16[8,256,384]{2,1,0:T(8,128)(2,1)} custom-call(s32[16]{0:T(128)} %frames_ref.3, s32[16]{0:T(128)} %get-tuple-element.44.slots_ref, bf16[2048,384]{1,0:T(8,128)(2,1)} %bitcast.58, bf16[2048,128]{1,0:T(8,128)(2,1)} %bitcast.61, f32[128,2048]{1,0:T(8,128)} %get-tuple-element.50.ot_ref, f32[8,512]{1,0:T(8,128)} %get-tuple-element.51.lse_ref, ...), custom_call_target="tpu_custom_call" | custom-call | flops 15000000512 | bytes 45000000 | tf_op jit(solution)/shard_map/attend_back/pallas_call | solution.py:693
  178.2 5.0 %all-to-all-start.3 = ((bf16[8,256,384]{2,1,0:T(8,128)(2,1)}), bf16[8,256,384]{2,1,0:T(8,128)(2,1)S(1)}, u32[]{:S(2)}, u32[]{:S(2)}) async-start(bf16[8,256,384]{2,1,0:T(8,128)(2,1)} %attend_back.1.after_ref), calls=%async_computation.3 | async-start | bytes 3145728 | tf_op jit(solution)/shard_map/all_to_all | solution.py:1207
  186.3 24.3 %collective-permute-done.3 = bf16[8,576,256]{2,1,0:T(8,128)(2,1)} collective-permute-done((bf16[8,576,256]{2,1,0:T(8,128)(2,1)}, bf16[8,576,256]{2,1,0:T(8,128)(2,1)}, u32[]{:S(2)}, u32[]{:S(2)}) %collective-permute-start.3) | collective-permute-done | bytes 2359328 | tf_op jit(solution)/shard_map/ppermute | solution.py:711
  210.6 37.5 %collective-permute-done.4.got_b = bf16[4,2,576,256]{3,2,1,0:T(8,128)(2,1)} collective-permute-done((bf16[4,2,576,256]{3,2,1,0:T(8,128)(2,1)}, bf16[4,2,576,256]{3,2,1,0:T(8,128)(2,1)}, u32[]{:S(2)}, u32[]{:S(2)}) %collective-permute-start.4) | collective-permute-done | bytes 2359328 | tf_op jit(solution)/shard_map/ppermute | solution.py:711
  248.1 6.9 %fold.3 = (bf16[4,576,256]{2,1,0:T(8,128)(2,1)}, bf16[4,576,256]{2,1,0:T(8,128)(2,1)}, bf16[4,576,256]{2,1,0:T(8,128)(2,1)}, bf16[4,576,256]{2,1,0:T(8,128)(2,1)}) custom-call(s32[2]{0:T(128)} %pad_add_fusion.3.bits_ref, bf16[4,2,576,256]{3,2,1,0:T(8,128)(2,1)} %bitcast.72, bf16[4,2,576,256]{3,2,1,0:T(8,128)(2,1)} %bitcast.13.got_a, ...), custom_call_target="tpu_custom_call" | custom-call | flops 5000000000 | bytes 15000000 | tf_op jit(solution)/shard_map/fold/pallas_call | solution.py:1094
  258.2 10.1 %first_back.1 = (bf16[256,1024]{1,0:T(8,128)(2,1)}, f32[2,2048]{1,0:T(2,128)}) custom-call(bf16[8,256,384]{2,1,0:T(8,128)(2,1)} %copy-done.2, bf16[256,1024]{1,0:T(8,128)(2,1)} %bitcast.69, f32[2,6144]{1,0:T(2,128)} %copy-done.6, f32[256,1024]{1,0:T(8,128)} %get-tuple-element.54.dmid_ref, bf16[1024,3072]{1,0:T(8,128)(2,1)} %vw_ref.3, ...), custom_call_target="tpu_custom_call" | custom-call | flops 8999999488 | bytes 27000000 | tf_op jit(solution)/shard_map/first_back/pallas_call | solution.py:991
  269.2 6.4 %qkv_parts.1 = (bf16[8,2,32,384]{3,2,1,0:T(8,128)(2,1)}, bf16[8,2,32,384]{3,2,1,0:T(8,128)(2,1)}) custom-call(s32[1]{0:T(128)} %bitcast.9.core_ref, bf16[2048,1024]{1,0:T(8,128)(2,1)} %all-gather.2.cloned.1.call-done.first_ref, bf16[2048,384]{1,0:T(8,128)(2,1)} %bitcast.59, f32[2,2048]{1,0:T(2,128)} %get-tuple-element.60.after_ref), custom_call_target="tpu_custom_call" | custom-call | flops 5000000000 | bytes 15000000 | tf_op jit(solution)/shard_map/qkv_parts/pallas_call | solution.py:1053
  288.6 4.6 %collective-permute-done.8 = bf16[8,2,6144]{2,1,0:T(2,128)(2,1)S(1)} collective-permute-done((bf16[8,2,6144]{2,1,0:T(2,128)(2,1)S(1)}, bf16[8,2,6144]{2,1,0:T(2,128)(2,1)S(1)}, u32[]{:S(2)}, u32[]{:S(2)}) %collective-permute-start.8) | collective-permute-done | bytes 196640 | tf_op jit(solution)/shard_map/ppermute | solution.py:711
  296.3 4.1 %all-to-all-start.4 = ((bf16[8,32,384]{2,1,0:T(8,128)(2,1)}), bf16[8,32,384]{2,1,0:T(8,128)(2,1)S(1)}, u32[]{:S(2)}, u32[]{:S(2)}) async-start(bf16[8,32,384]{2,1,0:T(8,128)(2,1)} %fusion.2), calls=%async_computation.4 | async-start | bytes 393216 | tf_op jit(solution)/shard_map/all_to_all | solution.py:1229
  301.5 4.2 %fold.4 = (bf16[2,576,256]{2,1,0:T(8,128)(2,1)}, bf16[2,576,256]{2,1,0:T(8,128)(2,1)}, bf16[2,576,256]{2,1,0:T(8,128)(2,1)}, bf16[2,576,256]{2,1,0:T(8,128)(2,1)}) custom-call(s32[2]{0:T(128)} %pad_add_fusion.5.bits_ref, bf16[2,2,576,256]{3,2,1,0:T(8,128)(2,1)} %bitcast.73, bf16[2,2,576,256]{3,2,1,0:T(8,128)(2,1)} %bitcast.63, ...), custom_call_target="tpu_custom_call" | custom-call | flops 3000000000 | bytes 9000000 | tf_op jit(solution)/shard_map/fold/pallas_call | solution.py:1094
  309.7 12.4 %collective-permute-done.14 = bf16[2,576,256]{2,1,0:T(8,128)(2,1)S(1)} collective-permute-done((bf16[2,576,256]{2,1,0:T(8,128)(2,1)}, bf16[2,576,256]{2,1,0:T(8,128)(2,1)S(1)}, u32[]{:S(2)}, u32[]{:S(2)}) %collective-permute-start.14) | collective-permute-done | bytes 589856 | tf_op jit(solution)/shard_map/ppermute | solution.py:711
  322.2 10.1 %collective-permute-done.15 = bf16[2,576,256]{2,1,0:T(8,128)(2,1)S(1)} collective-permute-done((bf16[2,576,256]{2,1,0:T(8,128)(2,1)}, bf16[2,576,256]{2,1,0:T(8,128)(2,1)S(1)}, u32[]{:S(2)}, u32[]{:S(2)}) %collective-permute-start.15) | collective-permute-done | bytes 589856 | tf_op jit(solution)/shard_map/ppermute | solution.py:711
  333.1 4.2 %fold.5 = (bf16[1,576,256]{2,1,0:T(8,128)(2,1)}, bf16[1,576,256]{2,1,0:T(8,128)(2,1)}, bf16[1,576,256]{2,1,0:T(8,128)(2,1)}, bf16[1,576,256]{2,1,0:T(8,128)(2,1)}) custom-call(s32[2]{0:T(128)} %pad_add_fusion.4.bits_ref, bf16[1,2,576,256]{3,2,1,0:T(8,128)(2,1)} %bitcast.75, bf16[1,2,576,256]{3,2,1,0:T(8,128)(2,1)} %bitcast.64, ...), custom_call_target="tpu_custom_call" | custom-call | flops 2000000000 | bytes 6000000 | tf_op jit(solution)/shard_map/fold/pallas_call | solution.py:1094
  344.4 14.1 %collective-permute-done.16 = bf16[1,576,256]{2,1,0:T(8,128)(2,1)S(1)} collective-permute-done((bf16[1,576,256]{2,1,0:T(8,128)(2,1)}, bf16[1,576,256]{2,1,0:T(8,128)(2,1)S(1)}, u32[]{:S(2)}, u32[]{:S(2)}) %collective-permute-start.16) | collective-permute-done | bytes 294944 | tf_op jit(solution)/shard_map/ppermute | solution.py:711
  358.5 5.4 %collective-permute-done.17 = bf16[1,576,256]{2,1,0:T(8,128)(2,1)S(1)} collective-permute-done((bf16[1,576,256]{2,1,0:T(8,128)(2,1)}, bf16[1,576,256]{2,1,0:T(8,128)(2,1)S(1)}, u32[]{:S(2)}, u32[]{:S(2)}) %collective-permute-start.17) | collective-permute-done | bytes 294944 | tf_op jit(solution)/shard_map/ppermute | solution.py:711
  (125 shorter events, 63.6 us)
Async XLA Ops:
  37.8 44.4 %all-to-all-start = ((bf16[8,256,384]{2,1,0:T(8,128)(2,1)}), bf16[8,256,384]{2,1,0:T(8,128)(2,1)S(1)}, u32[]{:S(2)}, u32[]{:S(2)}) async-start(bf16[8,256,384]{2,1,0:T(8,128)(2,1)} %get-tuple-element.45), calls=%async_computation | async-start | bytes 3145728 | tf_op jit(solution)/shard_map/all_to_all | solution.py:1189
  45.2 223.9 %all-gather.2.cloned.1.call-start = ((), (), s32[]{:S(2)}) async-start(), calls=%async_computation.5 | async-start | bytes 4718592 | tf_op jit(solution)/shard_map/all_gather | solution.py:1192
  45.5 1.4 collective-permute-start
  46.9 3.6 collective-permute-start.1
  133.2 10.5 %collective-permute-start.2 = (bf16[256,12288]{1,0:T(8,128)(2,1)}, bf16[256,12288]{1,0:T(8,128)(2,1)}, u32[]{:S(2)}, u32[]{:S(2)}) collective-permute-start(bf16[256,12288]{1,0:T(8,128)(2,1)} %get-tuple-element.52.mine_ref), channel_id=1, source_target_pairs={{0,1},{1,0},{2,3},{3,2},{4,5},{5,4},{6,7},{7,6},{8,9},{9,8},{10,11... | collective-permute-start | bytes 18874376 | tf_op jit(solution)/shard_map/ppermute | solution.py:711
  133.9 27.9 %all-to-all-start.2 = ((bf16[8,256,128]{2,1,0:T(8,128)(2,1)}), bf16[8,256,128]{2,1,0:T(8,128)(2,1)S(1)}, u32[]{:S(2)}, u32[]{:S(2)}) async-start(bf16[8,256,128]{2,1,0:T(8,128)(2,1)} %get-tuple-element.49), calls=%async_computation.2 | async-start | bytes 1048576 | tf_op jit(solution)/shard_map/all_to_all | solution.py:1202
  157.0 53.6 %collective-permute-start.3 = (bf16[8,576,256]{2,1,0:T(8,128)(2,1)}, bf16[8,576,256]{2,1,0:T(8,128)(2,1)}, u32[]{:S(2)}, u32[]{:S(2)}) collective-permute-start(bf16[8,576,256]{2,1,0:T(8,128)(2,1)} %get-tuple-element.53.after_ref), channel_id=1, source_target_pairs={{0,2},{1,3},{2,0},{3,1},{4,6},{5,7},{6,4},{7,5},{8,10},{9,11},{10,... | collective-permute-start | bytes 7077896 | tf_op jit(solution)/shard_map/ppermute | solution.py:711
  158.5 89.6 %collective-permute-start.4 = (bf16[4,2,576,256]{3,2,1,0:T(8,128)(2,1)}, bf16[4,2,576,256]{3,2,1,0:T(8,128)(2,1)}, u32[]{:S(2)}, u32[]{:S(2)}) collective-permute-start(bf16[4,2,576,256]{3,2,1,0:T(8,128)(2,1)} %get-tuple-element.57), channel_id=1, source_target_pairs={{0,4},{1,5},{2,6},{3,7},{4,0},{5,1},{6,2},{7,3},{8,12},{9,13},{10,... | collective-permute-start | bytes 7077896 | tf_op jit(solution)/shard_map/ppermute | solution.py:711
  178.2 78.8 %all-to-all-start.3 = ((bf16[8,256,384]{2,1,0:T(8,128)(2,1)}), bf16[8,256,384]{2,1,0:T(8,128)(2,1)S(1)}, u32[]{:S(2)}, u32[]{:S(2)}) async-start(bf16[8,256,384]{2,1,0:T(8,128)(2,1)} %attend_back.1.after_ref), calls=%async_computation.3 | async-start | bytes 3145728 | tf_op jit(solution)/shard_map/all_to_all | solution.py:1207
  255.0 45.5 %collective-permute-start.12 = (bf16[4,576,256]{2,1,0:T(8,128)(2,1)}, bf16[4,576,256]{2,1,0:T(8,128)(2,1)S(1)}, u32[]{:S(2)}, u32[]{:S(2)}) collective-permute-start(bf16[4,576,256]{2,1,0:T(8,128)(2,1)} %get-tuple-element.58.after_ref), channel_id=1, source_target_pairs={{0,4},{1,5},{2,6},{3,7},{4,0},{5,1},{6,2},{7,3},{8,12},{9,13},{10,... | collective-permute-start | bytes 3538952 | tf_op jit(solution)/shard_map/ppermute | solution.py:711
  256.4 44.0 %collective-permute-start.13 = (bf16[4,576,256]{2,1,0:T(8,128)(2,1)}, bf16[4,576,256]{2,1,0:T(8,128)(2,1)}, u32[]{:S(2)}, u32[]{:S(2)}) collective-permute-start(bf16[4,576,256]{2,1,0:T(8,128)(2,1)} %get-tuple-element.67), channel_id=1, source_target_pairs={{0,2},{1,3},{2,0},{3,1},{4,6},{5,7},{6,4},{7,5},{8,10},{9,11},{10,... | collective-permute-start | bytes 3538952 | tf_op jit(solution)/shard_map/ppermute | solution.py:711
  269.1 6.5 %collective-permute-start.5 = (bf16[1,2,6144]{2,1,0:T(2,128)(2,1)S(1)}, bf16[1,2,6144]{2,1,0:T(2,128)(2,1)S(1)}, u32[]{:S(2)}, u32[]{:S(2)}) collective-permute-start(bf16[1,2,6144]{2,1,0:T(2,128)(2,1)S(1)} %get-tuple-element.91), channel_id=1, source_target_pairs={{0,16},{1,17},{2,18},{3,19},{4,20},{5,21},{6,22},{7,23},{8,24},{9,... | collective-permute-start | bytes 73736 | tf_op jit(solution)/shard_map/ppermute | solution.py:711
  275.6 20.0 %copy-start.5 = (bf16[8,2,32,384]{3,2,1,0:T(8,128)(2,1)S(1)}, bf16[8,2,32,384]{3,2,1,0:T(8,128)(2,1)}, u32[]{:S(2)}) copy-start(bf16[8,2,32,384]{3,2,1,0:T(8,128)(2,1)} %get-tuple-element.63) | copy-start | bytes 1179652
  275.6 11.4 %collective-permute-start.10 = (bf16[8,2,32,384]{3,2,1,0:T(8,128)(2,1)}, bf16[8,2,32,384]{3,2,1,0:T(8,128)(2,1)S(1)}, u32[]{:S(2)}, u32[]{:S(2)}) collective-permute-start(bf16[8,2,32,384]{3,2,1,0:T(8,128)(2,1)} %get-tuple-element.64), channel_id=1, source_target_pairs={{0,1},{1,0},{2,3},{3,2},{4,5},{5,4},{6,7},{7,6},{8,9},{9,8},{10,11... | collective-permute-start | bytes 1179656 | tf_op jit(solution)/shard_map/ppermute | solution.py:711
  275.7 4.5 %collective-permute-start.6 = (bf16[2,2,6144]{2,1,0:T(2,128)(2,1)S(1)}, bf16[2,2,6144]{2,1,0:T(2,128)(2,1)S(1)}, u32[]{:S(2)}, u32[]{:S(2)}) collective-permute-start(bf16[2,2,6144]{2,1,0:T(2,128)(2,1)S(1)} %pad_maximum_fusion.2), channel_id=1, source_target_pairs={{0,8},{1,9},{2,10},{3,11},{4,12},{5,13},{6,14},{7,15},{8,0},{9,1},... | collective-permute-start | bytes 147464 | tf_op jit(solution)/shard_map/ppermute | solution.py:711
  280.3 4.8 %collective-permute-start.7 = (bf16[4,2,6144]{2,1,0:T(2,128)(2,1)S(1)}, bf16[4,2,6144]{2,1,0:T(2,128)(2,1)S(1)}, u32[]{:S(2)}, u32[]{:S(2)}) collective-permute-start(bf16[4,2,6144]{2,1,0:T(2,128)(2,1)S(1)} %pad_maximum_fusion.1), channel_id=1, source_target_pairs={{0,4},{1,5},{2,6},{3,7},{4,0},{5,1},{6,2},{7,3},{8,12},{9,13},{10,... | collective-permute-start | bytes 294920 | tf_op jit(solution)/shard_map/ppermute | solution.py:711
  285.3 7.8 %collective-permute-start.8 = (bf16[8,2,6144]{2,1,0:T(2,128)(2,1)S(1)}, bf16[8,2,6144]{2,1,0:T(2,128)(2,1)S(1)}, u32[]{:S(2)}, u32[]{:S(2)}) collective-permute-start(bf16[8,2,6144]{2,1,0:T(2,128)(2,1)S(1)} %pad_maximum_fusion), channel_id=1, source_target_pairs={{0,2},{1,3},{2,0},{3,1},{4,6},{5,7},{6,4},{7,5},{8,10},{9,11},{10,... | collective-permute-start | bytes 589832 | tf_op jit(solution)/shard_map/ppermute | solution.py:711
  288.0 7.6 %collective-permute-start.11 = (bf16[8,32,384]{2,1,0:T(8,128)(2,1)S(1)}, bf16[8,32,384]{2,1,0:T(8,128)(2,1)S(1)}, u32[]{:S(2)}, u32[]{:S(2)}) collective-permute-start(bf16[8,32,384]{2,1,0:T(8,128)(2,1)S(1)} %fusion.9), channel_id=1, source_target_pairs={{0,2},{1,3},{2,0},{3,1},{4,6},{5,7},{6,4},{7,5},{8,10},{9,11},{10,... | collective-permute-start | bytes 589832 | tf_op jit(solution)/shard_map/ppermute | solution.py:711
  293.4 14.4 %collective-permute-start.9 = (bf16[16,2,6144]{2,1,0:T(2,128)(2,1)S(1)}, bf16[16,2,6144]{2,1,0:T(2,128)(2,1)S(1)}, u32[]{:S(2)}, u32[]{:S(2)}) collective-permute-start(bf16[16,2,6144]{2,1,0:T(2,128)(2,1)S(1)} %get-tuple-element.81), channel_id=1, source_target_pairs={{0,1},{1,0},{2,3},{3,2},{4,5},{5,4},{6,7},{7,6},{8,9},{9,8},{10,11... | collective-permute-start | bytes 1179656 | tf_op jit(solution)/shard_map/ppermute | solution.py:711
  296.3 46.9 %all-to-all-start.4 = ((bf16[8,32,384]{2,1,0:T(8,128)(2,1)}), bf16[8,32,384]{2,1,0:T(8,128)(2,1)S(1)}, u32[]{:S(2)}, u32[]{:S(2)}) async-start(bf16[8,32,384]{2,1,0:T(8,128)(2,1)} %fusion.2), calls=%async_computation.4 | async-start | bytes 393216 | tf_op jit(solution)/shard_map/all_to_all | solution.py:1229
  305.7 16.5 %collective-permute-start.14 = (bf16[2,576,256]{2,1,0:T(8,128)(2,1)}, bf16[2,576,256]{2,1,0:T(8,128)(2,1)S(1)}, u32[]{:S(2)}, u32[]{:S(2)}) collective-permute-start(bf16[2,576,256]{2,1,0:T(8,128)(2,1)} %get-tuple-element.69), channel_id=1, source_target_pairs={{0,8},{1,9},{2,10},{3,11},{4,12},{5,13},{6,14},{7,15},{8,0},{9,1},... | collective-permute-start | bytes 1769480 | tf_op jit(solution)/shard_map/ppermute | solution.py:711
  307.7 24.6 %collective-permute-start.15 = (bf16[2,576,256]{2,1,0:T(8,128)(2,1)}, bf16[2,576,256]{2,1,0:T(8,128)(2,1)S(1)}, u32[]{:S(2)}, u32[]{:S(2)}) collective-permute-start(bf16[2,576,256]{2,1,0:T(8,128)(2,1)} %get-tuple-element.71), channel_id=1, source_target_pairs={{0,8},{1,9},{2,10},{3,11},{4,12},{5,13},{6,14},{7,15},{8,0},{9,1},... | collective-permute-start | bytes 1769480 | tf_op jit(solution)/shard_map/ppermute | solution.py:711
  337.3 21.2 %collective-permute-start.16 = (bf16[1,576,256]{2,1,0:T(8,128)(2,1)}, bf16[1,576,256]{2,1,0:T(8,128)(2,1)S(1)}, u32[]{:S(2)}, u32[]{:S(2)}) collective-permute-start(bf16[1,576,256]{2,1,0:T(8,128)(2,1)} %get-tuple-element.73), channel_id=1, source_target_pairs={{0,16},{1,17},{2,18},{3,19},{4,20},{5,21},{6,22},{7,23},{8,24},{9,... | collective-permute-start | bytes 884744 | tf_op jit(solution)/shard_map/ppermute | solution.py:711
  339.9 24.0 %collective-permute-start.17 = (bf16[1,576,256]{2,1,0:T(8,128)(2,1)}, bf16[1,576,256]{2,1,0:T(8,128)(2,1)S(1)}, u32[]{:S(2)}, u32[]{:S(2)}) collective-permute-start(bf16[1,576,256]{2,1,0:T(8,128)(2,1)} %get-tuple-element.75), channel_id=1, source_target_pairs={{0,16},{1,17},{2,18},{3,19},{4,20},{5,21},{6,22},{7,23},{8,24},{9,... | collective-permute-start | bytes 884744 | tf_op jit(solution)/shard_map/ppermute | solution.py:711
  (16 other events, 90.4 us)
Sparse Core Ops, SparseCore 0:
  134.0 115.4 all-gather.1
